TPU v7x, 256 devices: a whole 4x4x8 slice. The times are simulated.
256 devices in a mesh: ens: 8 (over z_lo, x), lat: 32 (over y, z_hi, core).
Axes of the slice: x: 4, y: 4, z: 8 (z_hi: 4, z_lo: 2; z = z_hi * 2 + z_lo), core: 2. Of those that a mesh axis runs over, the one named last changes fastest.
Arguments:
- members: float32 [160, 8, 64, 640], P('lat', 'ens'), may hold values from -24 to 24
- truth: float32 [4, 160, 64, 640], P(None, 'lat'), may hold values from -32 to 32
- target_time: int32 [160], P('lat'), may hold values from 0 to 3
- row_taps: int32 [1, 160, 5], P(None, 'lat'), may hold values from 0 to 159, as said below
- filters: float32 [1, 160, 5, 9, 5], P(None, 'lat'), may hold values from -1.2 to 1.2
- mixing: float32 [1, 64, 9, 64], replicated, may hold values from -0.25 to 0.25
Outputs:
- score_grad: float32 [160, 8, 64, 640], P('lat', 'ens')
- loss_value: float32 [1], replicated
Inputs may be any that keep to these rules, and one draw needn't show every extreme that they name: row_taps[l, i, t] lies within 4 rows of i; in every layer some row lists a row exactly 4 below it and some row one exactly 4 above it. `target_time`: selects one of the stored target fields for each latitude row.
All inputs are finite; a program needn't handle non-finite values.
Results may differ from a plain program's by a relative error of at most 0.0003.
Values sent between devices are 32-bit elements; how exact they have to be, the bound alone decides.
A program may use at most 64 MiB of HBM per device.

v0:
```python
import math

import jax
import jax.numpy as jnp
from jax import lax
from jax.sharding import Mesh
from jax.sharding import PartitionSpec as P

C = 64
NLON = 640
K = 9
LW = 5
REACH = 4
LAT = ("lat_0", "lat_1", "lat_2")
ENS = ("ens_0", "ens_1")
ENS_LAT = ("ens_0", "ens_1", "lat_0", "lat_1", "lat_2")


def padded(cells, sides, width):
    for axis, dim in sides:
        count = lax.axis_size(axis)
        ends = count - 1
        head = lax.slice_in_dim(cells, 0, width, axis=dim)
        tail = lax.slice_in_dim(cells, cells.shape[dim] - width, cells.shape[dim], axis=dim)
        cells = jnp.concatenate(
            [
                lax.ppermute(tail, axis, [(i, (i + 1) % count) for i in range(ends)]),
                cells,
                lax.ppermute(head, axis, [((i + 1) % count, i) for i in range(ends)]),
            ],
            axis=dim,
        )
    return cells


def split_up(x, dim, count):
    dims = x.shape
    tiles = x.reshape(*dims[:dim], count, dims[dim] // count, *dims[dim + 1 :])
    return jnp.moveaxis(tiles, dim, 0)


def cut_rows(length, count):
    unit = 8 if length >= 8 * count else 1
    return [length // unit * k // count * unit for k in range(1, count)]


def laid_out(tiles, dim):
    tiles = jnp.moveaxis(tiles, 0, dim)
    dims = tiles.shape
    return tiles.reshape(*dims[:dim], dims[dim] * dims[dim + 1], *dims[dim + 2 :])


def several_exchanges(x, axis, pieces, split_dim, concat_dim):
    tiles = split_up(x, split_dim, lax.axis_size(axis))
    cut = max(range(1, max(2, tiles.ndim - 1)), key=lambda d: tiles.shape[d])
    gathered = []
    for slab in jnp.split(tiles, cut_rows(tiles.shape[cut], pieces), axis=cut):
        if slab.size:
            gathered.append(lax.all_to_all(slab, axis, split_axis=0, concat_axis=0, tiled=True))
    return laid_out(jnp.concatenate(gathered, axis=cut), concat_dim)


def by_axis(x, axes):
    for axis in axes:
        x = lax.psum(x, axis)
    return x


def area_weights(total_rows, first_row, band_rows):
    latitude = (jnp.arange(total_rows, dtype=jnp.float32) + 0.5) * (
        math.pi / total_rows
    ) - 0.5 * math.pi
    cosine = jnp.cos(latitude)
    return lax.dynamic_slice_in_dim(cosine / jnp.mean(cosine), first_row, band_rows)


def score_cells(grouped, target_piece, area):
    total_members = grouped.shape[1]
    to_truth = grouped - target_piece[:, None]
    skill_dist = jnp.sqrt(jnp.mean(to_truth * to_truth, axis=2) + 1.0)

    def pair_terms(member):
        gap_field = member[:, None] - grouped
        distance = jnp.sqrt(jnp.mean(gap_field * gap_field, axis=2) + 1.0)
        return (jnp.sum(gap_field / distance[:, :, None], axis=1), jnp.sum(distance, axis=1))

    pull_sum, spread = lax.map(pair_terms, jnp.moveaxis(grouped, 1, 0))
    grad_piece = area[:, None, None, None] * (
        to_truth / skill_dist[:, :, None] - jnp.moveaxis(pull_sum, 0, 1) / total_members
    )
    per_cell = jnp.sum(skill_dist, axis=1) / total_members - jnp.sum(spread, axis=0) / (
        2.0 * total_members * total_members
    )
    return (grad_piece, jnp.sum(area[:, None] * per_cell))


def per_device(members, truth, target_time, row_taps, filters, mixing):
    highest = lax.Precision.HIGHEST
    band_rows = members.shape[0]
    own_count = members.shape[1]
    lon_cells = members.shape[3]
    half_width = LW // 2
    first_row = lax.axis_index(LAT) * band_rows
    total_rows = band_rows * lax.axis_size(LAT)
    extended_rows = band_rows + 2 * REACH
    fields = members
    extended = padded(fields, ((LAT, 0),), REACH)
    local_taps = row_taps[0] - (first_row - REACH)
    one_hot = (
        local_taps[:, :, None] == jnp.arange(extended_rows, dtype=jnp.int32)[None, None, :]
    ).astype(jnp.float32)
    coupling = jnp.einsum("rtkd,rtq->rkdq", filters[0], one_hot, precision=highest)
    shifted = jnp.stack(
        [jnp.roll(extended, half_width - lon_lag, axis=3) for lon_lag in range(LW)], axis=0
    )
    basis_out = jnp.dot(
        coupling.reshape(band_rows * K, LW * extended_rows),
        shifted.reshape(LW * extended_rows, -1),
        precision=highest,
        preferred_element_type=jnp.float32,
    )
    basis_out = basis_out.reshape(band_rows, K, own_count, C, lon_cells)
    mixed_out = jnp.einsum("okc,rkmcj->rmoj", mixing[0], basis_out, precision=highest)
    fields = fields + jax.nn.gelu(mixed_out, approximate=True)
    stored_count = truth.shape[0]
    selector = (target_time[None, :] == jnp.arange(stored_count, dtype=jnp.int32)[:, None]).astype(
        jnp.float32
    )
    target = jnp.sum(selector[:, :, None, None] * truth, axis=0)
    area = area_weights(total_rows, first_row, band_rows)
    piece_width = lon_cells // lax.axis_size(ENS)
    grouped = several_exchanges(fields, ENS, 2, 3, 1)
    target_piece = lax.dynamic_slice_in_dim(
        target, lax.axis_index(ENS) * piece_width, piece_width, 2
    )
    grad_piece, loss_part = score_cells(grouped, target_piece, area)
    score_grad = lax.all_to_all(grad_piece, ENS, split_axis=1, concat_axis=3, tiled=True)
    loss_value = by_axis(jnp.reshape(loss_part, (1,)), ENS_LAT) / (total_rows * NLON)
    return (score_grad, loss_value)


def solution(mesh):
    torus = Mesh(mesh.devices.reshape(2, 4, 4, 4, 2), ("ens_0", "ens_1", "lat_0", "lat_1", "lat_2"))
    placed = (
        P(LAT, ENS, None, None),
        P(None, LAT, None, None),
        P(LAT),
        P(None, LAT, None),
        P(None, LAT, None, None, None),
        P(),
    )
    return jax.shard_map(
        per_device,
        mesh=torus,
        in_specs=placed,
        out_specs=(P(LAT, ENS, None, None), P()),
        check_vma=False,
    )
```

profile of v0, /device:TPU:1, one launch (start us, length us, event | category | flops | bytes accessed | tf_op | source)
XLA Modules:
  0.0 171.9 jit_solution(8503414665143536271)
XLA Ops:
  0.7 1.5 fusion.40
  2.1 6.3 %collective-permute-start = (f32[4,1,64,640]{3,2,1,0:T(8,128)S(1)}, f32[4,1,64,640]{3,2,1,0:T(8,128)}, u32[]{:S(2)}, u32[]{:S(2)}) collective-permute-start(f32[4,1,64,640]{3,2,1,0:T(8,128)S(1)} %get-tuple-element.80), channel_id=1, source_target_pairs={{0,1},{1,2},{2,3},{3,4},{4,5},{5,6},{6,7},{7,8},{8,9},{9,10},{10,1... | collective-permute-start | bytes 1966088 | tf_op jit(solution)/shard_map/ppermute | solution.py:27
  8.4 1.9 %collective-permute-start.1 = (f32[4,1,64,640]{3,2,1,0:T(8,128)S(1)}, f32[4,1,64,640]{3,2,1,0:T(8,128)S(1)}, u32[]{:S(2)}, u32[]{:S(2)}) collective-permute-start(f32[4,1,64,640]{3,2,1,0:T(8,128)S(1)} %get-tuple-element.79), channel_id=1, source_target_pairs={{1,0},{2,1},{3,2},{4,3},{5,4},{6,5},{7,6},{8,7},{9,8},{10,9},{11,1... | collective-permute-start | bytes 1966088 | tf_op jit(solution)/shard_map/ppermute | solution.py:29
  10.4 0.4 convolution_bitcast_fusion
  11.0 7.0 %collective-permute-done = f32[4,1,64,640]{3,2,1,0:T(8,128)} collective-permute-done((f32[4,1,64,640]{3,2,1,0:T(8,128)S(1)}, f32[4,1,64,640]{3,2,1,0:T(8,128)}, u32[]{:S(2)}, u32[]{:S(2)}) %collective-permute-start) | collective-permute-done | bytes 655392 | tf_op jit(solution)/shard_map/ppermute | solution.py:27
  17.9 1.1 constant_dynamic-update-slice_fusion.2
  19.1 9.1 %collective-permute-done.1 = f32[4,1,64,640]{3,2,1,0:T(8,128)S(1)} collective-permute-done((f32[4,1,64,640]{3,2,1,0:T(8,128)S(1)}, f32[4,1,64,640]{3,2,1,0:T(8,128)S(1)}, u32[]{:S(2)}, u32[]{:S(2)}) %collective-permute-start.1) | collective-permute-done | bytes 655392 | tf_op jit(solution)/shard_map/ppermute | solution.py:29
  28.5 0.7 fusion.37
  29.4 0.6 slice.54
  30.1 0.6 fusion.6
  30.7 0.6 fusion.7
  31.5 0.3 fusion.8
  31.8 0.3 fusion.9
  32.1 4.7 %slice_bitcast_fusion = f32[64,640,65]{1,0,2:T(8,128)} fusion(f32[65,64,640]{2,1,0:T(8,128)S(1)} %bitcast.121), kind=kLoop, calls=%fused_computation.10 | loop fusion | bytes 21299200 | tf_op jit(solution)/shard_map/reshape.25
  36.8 23.5 %fusion.1 = f32[5,9,64,640]{3,0,2,1:T(8,128)S(1)} fusion(f32[5,9,65,1]{2,0,3,1:T(8,128)S(1)} %copy.79, f32[64,640,65]{1,0,2:T(8,128)} %slice_bitcast_fusion), kind=kOutput, calls=%fused_computation.7 | convolution fusion | flops 1437696000 | bytes 18034100 | tf_op jit(solution)/shard_map/dot_general | solution.py:116
  60.3 5.5 %fusion.23 = f32[5,1,64,640]{3,2,0,1:T(8,128)S(1)} fusion(f32[5,9,64,640]{3,0,2,1:T(8,128)S(1)} %fusion.1, f32[5,1,64,640]{3,2,1,0:T(8,128)S(1)} %copy-done.1, f32[1,64,9,64]{3,1,2,0:T(8,128)S(1)} %copy-done), kind=kOutput, calls=%fused_computation.37 | convolution fusion | flops 1417420800 | bytes 9158656 | tf_op jit(solution)/shard_map/okc,rkmcj->rmoj/dot_general | solution.py:123
  65.8 0.6 reshape.72
  66.4 0.3 copy.107
  66.7 1.2 fusion.39
  67.8 4.0 %all-to-all-start = ((f32[8,5,1,32,80]{4,3,1,2,0:T(8,128)}), f32[8,5,1,32,80]{4,3,1,2,0:T(8,128)S(1)}, u32[]{:S(2)}, u32[]{:S(2)}) async-start(f32[8,5,1,32,80]{4,3,1,2,0:T(8,128)} %get-tuple-element.78), calls=%async_computation | async-start | bytes 1310720 | tf_op jit(solution)/shard_map/all_to_all | solution.py:59
  71.9 0.7 fusion.35
  73.2 8.2 %all-to-all-done = f32[8,5,1,32,80]{4,3,1,2,0:T(8,128)S(1)} async-done(((f32[8,5,1,32,80]{4,3,1,2,0:T(8,128)}), f32[8,5,1,32,80]{4,3,1,2,0:T(8,128)S(1)}, u32[]{:S(2)}, u32[]{:S(2)}) %all-to-all-start) | async-done | bytes 409632 | tf_op jit(solution)/shard_map/all_to_all | solution.py:59
  81.3 3.5 %all-to-all-start.1 = ((f32[8,5,1,32,80]{4,3,1,2,0:T(8,128)}), f32[8,5,1,32,80]{4,3,1,2,0:T(8,128)S(1)}, u32[]{:S(2)}, u32[]{:S(2)}) async-start(f32[8,5,1,32,80]{4,3,1,2,0:T(8,128)} %get-tuple-element.77), calls=%async_computation.1 | async-start | bytes 1310720 | tf_op jit(solution)/shard_map/all_to_all | solution.py:59
  85.1 2.3 %multiply_reduce_fusion.1 = f32[5,64,640]{2,1,0:T(8,128)S(1)} fusion(f32[4,5,64,640]{3,2,1,0:T(8,128)} %param.9, f32[4,5]{1,0:T(4,128)S(1)} %fusion.33), kind=kLoop, calls=%fused_computation.13 | loop fusion | flops 1433600 | bytes 4096080 | tf_op jit(solution)/shard_map/reduce_sum | solution.py:129
  87.6 4.9 %all-to-all-done.1 = f32[8,5,1,32,80]{4,3,1,2,0:T(8,128)S(1)} async-done(((f32[8,5,1,32,80]{4,3,1,2,0:T(8,128)}), f32[8,5,1,32,80]{4,3,1,2,0:T(8,128)S(1)}, u32[]{:S(2)}, u32[]{:S(2)}) %all-to-all-start.1) | async-done | bytes 409632 | tf_op jit(solution)/shard_map/all_to_all | solution.py:59
  92.7 9.2 %while.12 = (s32[]{:T(128)}, f32[8,5,64,80]{3,2,1,0:T(8,128)}, f32[8,5,80]{2,1,0:T(8,128)S(1)}, f32[8,5,64,80]{3,2,1,0:T(8,128)S(1)}, f32[5,8,64,80]{3,2,1,0:T(8,128)S(1)}, /*index=5*/s32[]{:T(128)}) while((s32[]{:T(128)}, f32[8,5,64,80]{3,2,1,0:T(8,128)}, f32[8,5,80]{2,1,0:T(8,128)S(1)}, f32[8,5,64,80]{3,2,1,0:T(8,128)S(1)}, ...), condition=%wide.region_7.8_spmd, body=%wide.region_3.7_spmd.sunk | while | flops 1209202 | bytes 2478221 | solution.py:87
  92.7 0.2 multiply_reduce_fusion.5
  93.2 0.7 bitcast_dynamic-update-slice_fusion.5
  93.9 0.2 multiply_reduce_fusion.5
  94.3 0.7 bitcast_dynamic-update-slice_fusion.5
  95.0 0.2 multiply_reduce_fusion.5
  95.5 0.7 bitcast_dynamic-update-slice_fusion.5
  96.6 0.7 bitcast_dynamic-update-slice_fusion.5
  97.8 0.7 bitcast_dynamic-update-slice_fusion.5
  98.9 0.7 bitcast_dynamic-update-slice_fusion.5
  100.1 0.7 bitcast_dynamic-update-slice_fusion.5
  101.2 0.7 bitcast_dynamic-update-slice_fusion.5
  102.2 1.1 copy-done.2
  103.2 1.5 fusion.10
  104.7 3.6 %all-to-all-start.2 = ((f32[5,8,64,80]{3,2,0,1:T(8,128)}), f32[5,8,64,80]{3,2,0,1:T(8,128)S(1)}, u32[]{:S(2)}, u32[]{:S(2)}) async-start(f32[5,8,64,80]{3,2,0,1:T(8,128)} %fusion.10), calls=%async_computation.2 | async-start | bytes 2621440 | tf_op jit(solution)/shard_map/all_to_all | solution.py:137
  108.3 0.7 multiply_reduce_fusion.3
  108.9 9.5 %psum.35 = f32[1]{0:T(128)} all-reduce(f32[1]{0:T(128)} %bitcast.39), channel_id=1, replica_groups=mesh['ens_0'=2,'ens_1'=4,'lat_0'=4,'lat_1'=4,'lat_2'=2] {'ens_0'}, use_global_device_ids=true, to_apply=%region_11.12 | all-reduce | flops 1 | bytes 8 | tf_op jit(solution)/shard_map/psum | solution.py:65
  118.5 9.3 %psum.36 = f32[1]{0:T(128)} all-reduce(f32[1]{0:T(128)} %psum.35), channel_id=1, replica_groups=mesh['ens_0'=2,'ens_1'=4,'lat_0'=4,'lat_1'=4,'lat_2'=2] {'ens_1'}, use_global_device_ids=true, to_apply=%region_12.13 | all-reduce | flops 1 | bytes 8 | tf_op jit(solution)/shard_map/psum | solution.py:65
  127.8 20.1 %psum.37 = f32[1]{0:T(128)} all-reduce(f32[1]{0:T(128)} %psum.36), channel_id=1, replica_groups=mesh['ens_0'=2,'ens_1'=4,'lat_0'=4,'lat_1'=4,'lat_2'=2] {'lat_0'}, use_global_device_ids=true, to_apply=%region_13.14 | all-reduce | flops 1 | bytes 8 | tf_op jit(solution)/shard_map/psum | solution.py:65
  147.9 9.7 %psum.38 = f32[1]{0:T(128)} all-reduce(f32[1]{0:T(128)} %psum.37), channel_id=1, replica_groups=mesh['ens_0'=2,'ens_1'=4,'lat_0'=4,'lat_1'=4,'lat_2'=2] {'lat_1'}, use_global_device_ids=true, to_apply=%region_14.15 | all-reduce | flops 1 | bytes 8 | tf_op jit(solution)/shard_map/psum | solution.py:65
  157.7 10.4 %psum.39 = f32[1]{0:T(128)} all-reduce(f32[1]{0:T(128)} %psum.38), channel_id=1, replica_groups=mesh['ens_0'=2,'ens_1'=4,'lat_0'=4,'lat_1'=4,'lat_2'=2] {'lat_2'}, use_global_device_ids=true, to_apply=%region_15.16 | all-reduce | flops 1 | bytes 8 | tf_op jit(solution)/shard_map/psum | solution.py:65
  168.8 0.7 copy.76
  169.5 1.3 all_to_all.24
  (70 shorter events, 4.5 us)
Async XLA Ops:
  0.6 59.7 %copy-start = (f32[1,64,9,64]{3,1,2,0:T(8,128)S(1)}, f32[1,64,9,64]{3,1,2,0:T(8,128)}, u32[]{:S(2)}) copy-start(f32[1,64,9,64]{3,1,2,0:T(8,128)} %param.13) | copy-start | bytes 442372
  0.6 18.4 %copy-start.1 = (f32[5,1,64,640]{3,2,1,0:T(8,128)S(1)}, f32[5,1,64,640]{3,2,1,0:T(8,128)}, u32[]{:S(2)}) copy-start(f32[5,1,64,640]{3,2,1,0:T(8,128)} %param.8) | copy-start | bytes 2457604
  0.7 9.7 %copy-start.4 = (s32[1,5,5]{2,0,1:T(1,128)S(1)}, s32[1,5,5]{2,0,1:T(1,128)}, u32[]{:S(2)}) copy-start(s32[1,5,5]{2,0,1:T(1,128)} %param.11) | copy-start | bytes 304
  0.7 9.7 %copy-start.3 = (f32[1,5,5,9,5]{3,0,4,2,1:T(1,128)S(1)}, f32[1,5,5,9,5]{3,0,4,2,1:T(1,128)}, u32[]{:S(2)}) copy-start(f32[1,5,5,9,5]{3,0,4,2,1:T(1,128)} %param.12) | copy-start | bytes 13504
  2.1 15.8 %collective-permute-start = (f32[4,1,64,640]{3,2,1,0:T(8,128)S(1)}, f32[4,1,64,640]{3,2,1,0:T(8,128)}, u32[]{:S(2)}, u32[]{:S(2)}) collective-permute-start(f32[4,1,64,640]{3,2,1,0:T(8,128)S(1)} %get-tuple-element.80), channel_id=1, source_target_pairs={{0,1},{1,2},{2,3},{3,4},{4,5},{5,6},{6,7},{7,8},{8,9},{9,10},{10,1... | collective-permute-start | bytes 1966088 | tf_op jit(solution)/shard_map/ppermute | solution.py:27
  8.4 19.8 %collective-permute-start.1 = (f32[4,1,64,640]{3,2,1,0:T(8,128)S(1)}, f32[4,1,64,640]{3,2,1,0:T(8,128)S(1)}, u32[]{:S(2)}, u32[]{:S(2)}) collective-permute-start(f32[4,1,64,640]{3,2,1,0:T(8,128)S(1)} %get-tuple-element.79), channel_id=1, source_target_pairs={{1,0},{2,1},{3,2},{4,3},{5,4},{6,5},{7,6},{8,7},{9,8},{10,9},{11,1... | collective-permute-start | bytes 1966088 | tf_op jit(solution)/shard_map/ppermute | solution.py:29
  66.7 18.4 %copy-start.5 = (s32[5]{0:T(128)S(1)}, s32[5]{0:T(128)}, u32[]{:S(2)}) copy-start(s32[5]{0:T(128)} %param.10) | copy-start | bytes 64
  67.8 13.5 %all-to-all-start = ((f32[8,5,1,32,80]{4,3,1,2,0:T(8,128)}), f32[8,5,1,32,80]{4,3,1,2,0:T(8,128)S(1)}, u32[]{:S(2)}, u32[]{:S(2)}) async-start(f32[8,5,1,32,80]{4,3,1,2,0:T(8,128)} %get-tuple-element.78), calls=%async_computation | async-start | bytes 1310720 | tf_op jit(solution)/shard_map/all_to_all | solution.py:59
  81.3 11.1 %all-to-all-start.1 = ((f32[8,5,1,32,80]{4,3,1,2,0:T(8,128)}), f32[8,5,1,32,80]{4,3,1,2,0:T(8,128)S(1)}, u32[]{:S(2)}, u32[]{:S(2)}) async-start(f32[8,5,1,32,80]{4,3,1,2,0:T(8,128)} %get-tuple-element.77), calls=%async_computation.1 | async-start | bytes 1310720 | tf_op jit(solution)/shard_map/all_to_all | solution.py:59
  101.9 1.3 copy-start.2
  104.7 64.1 %all-to-all-start.2 = ((f32[5,8,64,80]{3,2,0,1:T(8,128)}), f32[5,8,64,80]{3,2,0,1:T(8,128)S(1)}, u32[]{:S(2)}, u32[]{:S(2)}) async-start(f32[5,8,64,80]{3,2,0,1:T(8,128)} %fusion.10), calls=%async_computation.2 | async-start | bytes 2621440 | tf_op jit(solution)/shard_map/all_to_all | solution.py:137
where the time goes:
time: 173 us; the launch traced here: 172 us
  blocking collectives  59.1 us (34%)
  matrix products  29.4 us (17%)
  waiting for transfers between devices  29.2 us (17%)
  local copies, waits for them, and re-layouts  20.6 us (12%)
  starting transfers between devices  19.3 us (11%)
  other arithmetic  10.7 us (6%)
  between operations  3.41 us (2%)
    psum x5, blocking collectives, by_axis(): x = lax.psum(x, axis)  59.1 us
    dot_general x1, matrix products, per_device(): jnp.dot(coupling.reshape(band_rows * K, LW * extended_rows), shifted.resh...  23.5 us
    all_to_all x2, waiting for transfers between devices, several_exchanges(): lax.all_to_all(slab, axis, split_axis=0, concat_axis=0, tiled=True)  13.1 us
    ppermute x1, waiting for transfers between devices, padded(): lax.ppermute(head, axis, [((i + 1) % count, i) for i in range(ends)])  9.12 us
    all_to_all x2, starting transfers between devices, several_exchanges(): lax.all_to_all(slab, axis, split_axis=0, concat_axis=0, tiled=True)  7.56 us
    ppermute x1, waiting for transfers between devices, padded(): lax.ppermute(tail, axis, [(i, (i + 1) % count) for i in range(ends)])  6.96 us
    ppermute x1, starting transfers between devices, padded(): lax.ppermute(tail, axis, [(i, (i + 1) % count) for i in range(ends)])  6.29 us
    dot_general x1, matrix products, per_device(): jnp.einsum('okc,rkmcj->rmoj', mixing[0], basis_out, precision=highest)  5.48 us
  transfers between devices with their start and end apart: 5, of which 4 were waited for; matrix products, arithmetic and copies ran while one was open for 3% of the time, Pallas kernels for 0%

commit v1 on v0

v1 whole, which is shorter than its diff:
```python
import functools
import math

import jax
import jax.numpy as jnp
from jax import lax
from jax.experimental import pallas as pl
from jax.experimental.pallas import tpu as pltpu
from jax.sharding import PartitionSpec as P

C = 64
NLON = 640
K = 9
KP = 16
TAPS = 5
LW = 5
REACH = 4
ROWS = 5
LANE = 128
NB = NLON // LANE
BLOCKS = ROWS * NB
SIDE = REACH * C
OWN = ROWS * C
OWN_PAD = 384
BAND = LW * C
MESH = pl.DeviceIdType.MESH
CHUNKS = ((0, 256), (256, 256), (512, 128))
F32 = jnp.float32
BF16 = jnp.bfloat16


def split(x):
    hi = x.astype(BF16)
    return hi, (x - hi.astype(F32)).astype(BF16)


def dot3(w_hi, w_lo, x_hi, x_lo):
    dot = functools.partial(jnp.dot, preferred_element_type=F32)
    return dot(w_hi, x_hi) + dot(w_hi, x_lo) + dot(w_lo, x_hi)


def block_place(b):
    return lax.rem(b, ROWS), lax.rem(b // ROWS + 1, NB)


def kernel(
    n_ens,
    n_lat,
    taps_ref,
    time_ref,
    area_ref,
    filt_ref,
    mix_ref,
    members_ref,
    truth_ref,
    out_ref,
    loss_ref,
    own,
    halo,
    own_hi,
    own_lo,
    side_hi,
    side_lo,
    mdup,
    a_own,
    a_side,
    w_own_hi,
    w_own_lo,
    w_side_hi,
    w_side_lo,
    acc,
    states,
    recv,
    grads,
    cand,
    target,
    lossbuf1,
    lossbuf2,
    lossbuf3,
    own_sem,
    cand_sem,
    halo_send,
    halo_recv,
    fwd_send,
    fwd_recv,
    back_send,
    back_recv,
    self_sem,
    l1_send,
    l1_recv,
    l2_send,
    l2_recv,
    l3_send,
    l3_recv,
):
    me = lax.axis_index("ens")
    lat = lax.axis_index("lat")
    group = min(8, n_lat)
    tall = n_lat // group
    first = lat * ROWS
    core = lax.rem(lat, 2)
    near = 1 - core
    far = core
    slots = BLOCKS // n_ens
    extra = lax.rem(core * (n_ens // 2) + lax.rem(lat // 2, n_ens // 2), n_ens)
    inner = lax.rem(lat, group)
    outer = lat // group
    has_up = lat < n_lat - 1
    has_down = lat > 0

    def place(ens_at, lat_at):
        return {"ens": ens_at, "lat": lat_at}

    def ens_peer(k):
        return lax.rem(me + k, n_ens)

    def inner_peer(k):
        return outer * group + lax.rem(inner + k, group)

    def outer_peer(k):
        return lax.rem(outer + k, tall) * group + inner

    own_copy = pltpu.make_async_copy(members_ref.at[:, 0], own, own_sem)
    own_copy.start()

    def cand_copy(s):
        r, lon = block_place(n_ens * s + me)
        return pltpu.make_async_copy(
            truth_ref.at[:, r, :, pl.ds(pl.multiple_of(lon * LANE, LANE), LANE)], cand.at[s], cand_sem.at[s]
        )

    for s in range(slots):
        cand_copy(s).start()

    @pl.when(me == extra)
    def _():
        r, lon = ROWS - 1, 0
        pltpu.make_async_copy(truth_ref.at[:, r, :, pl.ds(lon, LANE)], cand.at[slots], cand_sem.at[slots]).start()

    barrier = pltpu.get_barrier_semaphore()
    for k in range(1, n_ens):
        pl.semaphore_signal(barrier, inc=1, device_id=place(ens_peer(k), lat), device_id_type=MESH)
    for k in range(1, group):
        pl.semaphore_signal(barrier, inc=1, device_id=place(me, inner_peer(k)), device_id_type=MESH)
    for k in range(1, tall):
        pl.semaphore_signal(barrier, inc=1, device_id=place(me, outer_peer(k)), device_id_type=MESH)
    over_up = has_up & (inner == group - 1)
    over_down = has_down & (inner == 0)

    @pl.when(over_up)
    def _():
        pl.semaphore_signal(barrier, inc=1, device_id=place(me, lat + 1), device_id_type=MESH)

    @pl.when(over_down)
    def _():
        pl.semaphore_signal(barrier, inc=1, device_id=place(me, lat - 1), device_id_type=MESH)

    greeted = n_ens - 1 + group - 1 + tall - 1
    pl.semaphore_wait(barrier, greeted + over_up.astype(jnp.int32) + over_down.astype(jnp.int32))

    def halo_copy(side, chunk):
        start, width = CHUNKS[chunk]
        rows = pl.ds(1, REACH) if side == 0 else pl.ds(0, REACH)
        to = lat + 1 if side == 0 else lat - 1
        return pltpu.make_async_remote_copy(
            src_ref=members_ref.at[rows, 0, :, pl.ds(start, width)],
            dst_ref=halo.at[side, :, :, pl.ds(start, width)],
            send_sem=halo_send.at[side, chunk],
            recv_sem=halo_recv.at[side, chunk],
            device_id=place(me, to),
            device_id_type=MESH,
        )

    def send_side(side):
        for chunk in range(len(CHUNKS)):
            halo_copy(side, chunk).start()

    @pl.when((core == 1) & has_up)
    def _():
        send_side(0)

    @pl.when((core == 0) & has_down)
    def _():
        send_side(1)

    @pl.when((core == 0) & has_up)
    def _():
        send_side(0)

    @pl.when((core == 1) & has_down)
    def _():
        send_side(1)

    @pl.when(jnp.logical_not(has_down))
    def _():
        halo[0] = jnp.zeros_like(halo[0])

    @pl.when(jnp.logical_not(has_up))
    def _():
        halo[1] = jnp.zeros_like(halo[1])

    for k in range(K):
        mdup[k] = jnp.concatenate([mix_ref[k], mix_ref[k]], axis=1)

    def row_of(width, low, high):
        lane = lax.broadcasted_iota(jnp.int32, (1, width), 1)
        q = low + lane // C
        return jnp.where(q < high, q, -1)

    q_own = row_of(OWN_PAD, REACH, REACH + ROWS)
    q_sides = (row_of(SIDE, 0, REACH), row_of(SIDE, REACH + ROWS, ROWS + 2 * REACH))

    def spread(r, q):
        total = None
        for t in range(TAPS):
            hit = (q == taps_ref[r * TAPS + t] - first + REACH).astype(F32)
            term = filt_ref[r, :, t : t + 1] * hit
            total = term if total is None else total + term
        return total

    @pl.loop(0, ROWS)
    def _(r):
        wide = spread(r, q_own)
        low = spread(r, q_sides[0])
        high = spread(r, q_sides[1])
        for d in range(LW):
            a_own[r * LW + d] = wide[d * KP : (d + 1) * KP]
            a_side[0, r * LW + d] = low[d * KP : (d + 1) * KP]
            a_side[1, r * LW + d] = high[d * KP : (d + 1) * KP]

    def weights(rd, a_at, width):
        for at in range(0, width, LANE):
            total = None
            for k in range(K):
                term = a_at[rd, k : k + 1, at : at + LANE] * mdup[k]
                total = term if total is None else total + term
            yield at, split(total)

    @pl.loop(0, ROWS * LW)
    def _(rd):
        rows = pl.ds(pl.multiple_of(rd * C, C), C)
        for at, (hi, lo) in weights(rd, a_own, OWN_PAD):
            w_own_hi[rows, at : at + LANE] = hi
            w_own_lo[rows, at : at + LANE] = lo

    own_copy.wait()
    hi, lo = split(own[...].reshape(OWN, NLON))
    own_hi[:OWN] = hi
    own_lo[:OWN] = lo
    own_hi[OWN:] = jnp.zeros((OWN_PAD - OWN, NLON), BF16)
    own_lo[OWN:] = jnp.zeros((OWN_PAD - OWN, NLON), BF16)

    @pl.loop(0, ROWS)
    def _(r):
        rows = pl.ds(pl.multiple_of(r * BAND, BAND), BAND)
        for start, width in CHUNKS:
            lons = pl.ds(start, width)
            acc[rows, lons] = dot3(w_own_hi[rows, :], w_own_lo[rows, :], own_hi[:, lons], own_lo[:, lons])

    def side_weights(side):
        a_at = a_side.at[side]

        @pl.loop(0, REACH * LW)
        def _(i):
            rows = pl.ds(pl.multiple_of(i * C, C), C)
            for at, (hi, lo) in weights(i + side * LW, a_at, SIDE):
                w_side_hi[rows, at : at + LANE] = hi
                w_side_lo[rows, at : at + LANE] = lo

    def wait_halo(side, chunk):
        @pl.when((side == 0) & has_down)
        def _():
            halo_copy(0, chunk).wait_recv()

        @pl.when((side == 1) & has_up)
        def _():
            halo_copy(1, chunk).wait_recv()

    def add_side(side, chunk):
        start, width = CHUNKS[chunk]
        lons = pl.ds(start, width)
        hi, lo = split(halo[side, :, :, lons].reshape(SIDE, width))
        side_hi[:, lons] = hi
        side_lo[:, lons] = lo

        @pl.loop(0, REACH)
        def _(i):
            rows = pl.ds(pl.multiple_of(i * BAND, BAND), BAND)
            acc_rows = pl.ds(pl.multiple_of((i + side) * BAND, BAND), BAND)
            acc[acc_rows, lons] += dot3(w_side_hi[rows, :], w_side_lo[rows, :], side_hi[:, lons], side_lo[:, lons])

    side_weights(near)
    for chunk in range(len(CHUNKS)):
        wait_halo(near, chunk)
        add_side(near, chunk)
    side_weights(far)

    def pick_target(s, r):
        time = time_ref[r]
        picked = cand[s, 0]
        for t in range(1, 4):
            picked = jnp.where(time == t, cand[s, t], picked)
        target[s] = picked

    for s in range(slots):
        cand_copy(s).wait()
        pick_target(s, lax.rem(n_ens * s + me, ROWS))

    @pl.when(me == extra)
    def _():
        pltpu.make_async_copy(truth_ref.at[:, ROWS - 1, :, pl.ds(0, LANE)], cand.at[slots], cand_sem.at[slots]).wait()
        pick_target(slots, ROWS - 1)

    lane = lax.broadcasted_iota(jnp.int32, (C, LANE), 1)

    def finish(lon, first_block):
        @pl.loop(0, ROWS)
        def _(r):
            def part(d, at):
                rows = pl.ds(pl.multiple_of(r * BAND + d * C, C), C)
                return acc[rows, at * LANE : (at + 1) * LANE]

            total = part(2, lon)
            for d in (0, 1, 3, 4):
                shift = d - LW // 2
                if shift > 0:
                    mine = jnp.where(lane < shift, part(d, (lon + 1) % NB), part(d, lon))
                else:
                    mine = jnp.where(lane >= LANE + shift, part(d, (lon - 1) % NB), part(d, lon))
                total = total + pltpu.roll(mine, (-shift) % LANE, 1)
            cube = total + 0.044715 * total * total * total
            gelu = 0.5 * total * (1.0 + jnp.tanh(math.sqrt(2.0 / math.pi) * cube))
            states[first_block + r] = own[r, :, lon * LANE : (lon + 1) * LANE] + gelu

    def fwd_copy(s, to, source):
        return pltpu.make_async_remote_copy(
            src_ref=states.at[n_ens * s + to] if s < slots else states.at[BLOCKS - 1],
            dst_ref=recv.at[s, source],
            send_sem=fwd_send.at[s, to],
            recv_sem=fwd_recv.at[s, source],
            device_id=place(to, lat),
            device_id_type=MESH,
        )

    def send_slot(s):
        for k in range(1, n_ens):
            fwd_copy(s, ens_peer(k), me).start()
        recv[s, me] = states[n_ens * s + me]

    for chunk in (0, 1):
        wait_halo(far, chunk)
        add_side(far, chunk)
    finish(1, 0)
    finish(2, 5)
    send_slot(0)
    wait_halo(far, 2)
    add_side(far, 2)
    finish(3, 10)
    for s in range(1, slots):
        if n_ens * (s + 1) <= 15:
            send_slot(s)
    finish(4, 15)
    finish(0, 20)
    for s in range(1, slots):
        if n_ens * (s + 1) > 15:
            send_slot(s)

    @pl.when(me != extra)
    def _():
        fwd_copy(slots, extra, me).start()

    pairs = [(a, b) for a in range(n_ens) for b in range(a + 1, n_ens)]

    def back_copy(s, b, r, lon, to):
        return pltpu.make_async_remote_copy(
            src_ref=grads.at[s, to],
            dst_ref=out_ref.at[r, 0, :, pl.ds(pl.multiple_of(lon * LANE, LANE), LANE)],
            send_sem=back_send.at[s, to],
            recv_sem=back_recv.at[b],
            device_id=place(to, lat),
            device_id_type=MESH,
        )

    def self_copy(s, r, lon):
        return pltpu.make_async_copy(
            grads.at[s, me],
            out_ref.at[r, 0, :, pl.ds(pl.multiple_of(lon * LANE, LANE), LANE)],
            self_sem.at[s],
        )

    def score(s, b):
        r, lon = block_place(b)
        for k in range(1, n_ens):
            fwd_copy(s, me, ens_peer(k)).wait_recv()
        area = area_ref[first + r]

        def square(v, sums):
            rows = pl.ds(pl.multiple_of(v * 8, 8), 8)
            x = [recv[s, m, rows, :] for m in range(n_ens)]
            goal = target[s, rows, :]
            gaps = [xm - goal for xm in x] + [x[a] - x[c] for a, c in pairs]
            return tuple(total + gap * gap for total, gap in zip(sums, gaps))

        zero = jnp.zeros((8, LANE), F32)
        sums = lax.fori_loop(0, C // 8, square, (zero,) * (n_ens + len(pairs)))
        scaled = []
        skill_sum = jnp.zeros((1, LANE), F32)
        pair_sum = jnp.zeros((1, LANE), F32)
        for at, total in enumerate(sums):
            mean = jnp.sum(total, axis=0, keepdims=True) * (1.0 / C) + 1.0
            inverse = lax.rsqrt(mean)
            if at < n_ens:
                skill_sum = skill_sum + mean * inverse
                scaled.append(jnp.broadcast_to(inverse * area, (8, LANE)))
            else:
                pair_sum = pair_sum + mean * inverse
                scaled.append(jnp.broadcast_to(inverse * (area * (1.0 / n_ens)), (8, LANE)))
        cell = skill_sum * (1.0 / n_ens) - (2.0 * pair_sum + n_ens) * (1.0 / (2 * n_ens * n_ens))

        @pl.loop(0, C // 8)
        def _(v):
            rows = pl.ds(pl.multiple_of(v * 8, 8), 8)
            x = [recv[s, m, rows, :] for m in range(n_ens)]
            goal = target[s, rows, :]
            g = [(x[m] - goal) * scaled[m] for m in range(n_ens)]
            for at, (a, c) in enumerate(pairs):
                pull = (x[a] - x[c]) * scaled[n_ens + at]
                g[a] = g[a] - pull
                g[c] = g[c] + pull
            for m in range(n_ens):
                grads[s, m, rows, :] = g[m]

        for k in range(1, n_ens):
            back_copy(s, b, r, lon, ens_peer(k)).start()
        self_copy(s, r, lon).start()
        return jnp.broadcast_to(area * cell, (8, LANE))

    part = score(0, me)
    for s in range(1, slots):
        part = part + score(s, n_ens * s + me)
    lossbuf1[me] = part

    @pl.when(me == extra)
    def _():
        recv[slots, me] = states[BLOCKS - 1]
        lossbuf1[me] += score(slots, BLOCKS - 1)

    def level(buf, send, got, count, mine, peer):
        def copy(k, slot):
            return pltpu.make_async_remote_copy(
                src_ref=buf.at[mine],
                dst_ref=buf.at[slot],
                send_sem=send.at[k],
                recv_sem=got.at[slot],
                device_id=peer(k),
                device_id_type=MESH,
            )

        for k in range(1, count):
            copy(k, mine).start()
        for k in range(1, count):
            copy(k, lax.rem(mine + k, count)).wait_recv()
        total = buf[0]
        for k in range(1, count):
            total = total + buf[k]
        return total, lambda: [copy(k, mine).wait_send() for k in range(1, count)]

    total, done1 = level(lossbuf1, l1_send, l1_recv, n_ens, me, lambda k: place(ens_peer(k), lat))
    lossbuf2[inner] = total
    total, done2 = level(lossbuf2, l2_send, l2_recv, group, inner, lambda k: place(me, inner_peer(k)))
    lossbuf3[outer] = total
    total, done3 = level(lossbuf3, l3_send, l3_recv, tall, outer, lambda k: place(me, outer_peer(k)))
    loss_ref[0] = jnp.sum(total[0:1, :]) * (1.0 / (n_lat * ROWS * NLON))

    def wait_back(b, owner):
        @pl.when(me != owner)
        def _():
            r, lon = block_place(b)
            back_copy(0, b, r, lon, me).wait_recv()

    for s in range(slots):
        b = n_ens * s + me
        self_copy(s, *block_place(b)).wait()
        for k in range(1, n_ens):
            to = ens_peer(k)
            c = n_ens * s + to
            back_copy(s, c, *block_place(c), me).wait_recv()
            back_copy(s, b, *block_place(b), to).wait_send()
            fwd_copy(s, to, me).wait_send()
    last = BLOCKS - 1

    @pl.when(me == extra)
    def _():
        self_copy(slots, *block_place(last)).wait()
        for k in range(1, n_ens):
            back_copy(slots, last, *block_place(last), ens_peer(k)).wait_send()

    @pl.when(me != extra)
    def _():
        back_copy(slots, last, *block_place(last), me).wait_recv()
        fwd_copy(slots, extra, me).wait_send()

    for done in (done1, done2, done3):
        done()

    def sent(side, there):
        @pl.when(there)
        def _():
            for chunk in range(len(CHUNKS)):
                halo_copy(side, chunk).wait_send()

    sent(0, has_up)
    sent(1, has_down)


def area_weights(total_rows):
    latitude = (jnp.arange(total_rows, dtype=F32) + 0.5) * (math.pi / total_rows) - 0.5 * math.pi
    cosine = jnp.cos(latitude)
    return cosine / jnp.mean(cosine)


def per_device(n_ens, n_lat, members, truth, target_time, row_taps, filters, mixing):
    taps = row_taps.reshape(ROWS * TAPS)
    spread = jnp.transpose(filters[0], (0, 3, 2, 1)).reshape(1, ROWS, LW, K, TAPS)[0]
    spread = jnp.pad(spread, ((0, 0), (0, 0), (0, KP - K), (0, 0))).reshape(ROWS, LW * KP, TAPS)
    mix = jnp.transpose(mixing[0], (1, 0, 2))
    area = area_weights(n_lat * ROWS)
    slots = BLOCKS // n_ens
    group = min(8, n_lat)
    tall = n_lat // group
    vmem = pltpu.VMEM
    dma = pltpu.SemaphoreType.DMA
    smem_spec = pl.BlockSpec(memory_space=pltpu.SMEM)
    vmem_spec = pl.BlockSpec(memory_space=pltpu.VMEM)
    any_spec = pl.BlockSpec(memory_space=pl.ANY)
    return pl.pallas_call(
        functools.partial(kernel, n_ens, n_lat),
        out_shape=(
            jax.ShapeDtypeStruct((ROWS, 1, C, NLON), F32),
            jax.ShapeDtypeStruct((1,), F32),
        ),
        in_specs=[smem_spec, smem_spec, smem_spec, vmem_spec, vmem_spec, any_spec, any_spec],
        out_specs=(any_spec, smem_spec),
        scratch_shapes=[
            vmem((ROWS, C, NLON), F32),
            vmem((2, REACH, C, NLON), F32),
            vmem((OWN_PAD, NLON), BF16),
            vmem((OWN_PAD, NLON), BF16),
            vmem((SIDE, NLON), BF16),
            vmem((SIDE, NLON), BF16),
            vmem((K, C, LANE), F32),
            vmem((ROWS * LW, KP, OWN_PAD), F32),
            vmem((2, ROWS * LW, KP, SIDE), F32),
            vmem((ROWS * BAND, OWN_PAD), BF16),
            vmem((ROWS * BAND, OWN_PAD), BF16),
            vmem((REACH * BAND, SIDE), BF16),
            vmem((REACH * BAND, SIDE), BF16),
            vmem((ROWS * BAND, NLON), F32),
            vmem((BLOCKS, C, LANE), F32),
            vmem((slots + 1, n_ens, C, LANE), F32),
            vmem((slots + 1, n_ens, C, LANE), F32),
            vmem((slots + 1, 4, C, LANE), F32),
            vmem((slots + 1, C, LANE), F32),
            vmem((n_ens, 8, LANE), F32),
            vmem((group, 8, LANE), F32),
            vmem((tall, 8, LANE), F32),
            dma,
            dma((slots + 1,)),
            dma((2, len(CHUNKS))),
            dma((2, len(CHUNKS))),
            dma((slots + 1, n_ens)),
            dma((slots + 1, n_ens)),
            dma((slots + 1, n_ens)),
            dma((BLOCKS,)),
            dma((slots + 1,)),
            dma((n_ens,)),
            dma((n_ens,)),
            dma((group,)),
            dma((group,)),
            dma((tall,)),
            dma((tall,)),
        ],
        compiler_params=pltpu.CompilerParams(
            collective_id=0, has_side_effects=True, vmem_limit_bytes=60 * 2**20
        ),
        cost_estimate=pl.CostEstimate(flops=5_000_000_000, bytes_accessed=4_000_000, transcendentals=400_000),
    )(taps, target_time, area, spread, mix, members, truth)


def solution(mesh):
    placed = (
        P("lat", "ens", None, None),
        P(None, "lat", None, None),
        P("lat"),
        P(None, "lat", None),
        P(None, "lat", None, None, None),
        P(),
    )
    return jax.shard_map(
        functools.partial(per_device, mesh.shape["ens"], mesh.shape["lat"]),
        mesh=mesh,
        in_specs=placed,
        out_specs=(P("lat", "ens", None, None), P()),
        check_vma=False,
    )
```

time: 173 us -> 71 us (0.41)
  Pallas kernels: 0 us -> 61.2 us
  blocking collectives: 59.1 us -> 0 us
  matrix products: 29.4 us -> 0 us
  waiting for transfers between devices: 29.2 us -> 0 us
  starting transfers between devices: 19.3 us -> 0 us
  local copies, waits for them, and re-layouts: 20.6 us -> 4.48 us
  other arithmetic: 10.7 us -> 1.96 us
    pallas_call x0 -> x1, Pallas kernels: none -> 61.2 us  [per_device(): pl.pallas_call(functools.partial(kernel, n_ens, n_lat), out_shape=(jax.Sh...]
    psum x5 -> x0, blocking collectives: 59.1 us -> none  [by_axis(): x = lax.psum(x, axis)]
    dot_general x3 -> x0, matrix products: 29.4 us -> none  [the longest x1 23.5 us: per_device(): jnp.dot(coupling.reshape(band_rows * K, LW * extended_rows), shifted.resh...]
    ppermute x2 -> x0, waiting for transfers between devices: 16.1 us -> none  [the longest x1 9.12 us: padded(): lax.ppermute(head, axis, [((i + 1) % count, i) for i in range(ends)])]
    all_to_all x3 -> x0, waiting for transfers between devices: 13.1 us -> none  [the longest x2 13.1 us: several_exchanges(): lax.all_to_all(slab, axis, split_axis=0, concat_axis=0, tiled=True)]
    all_to_all x3 -> x0, starting transfers between devices: 11.1 us -> none  [the longest x2 7.56 us: several_exchanges(): lax.all_to_all(slab, axis, split_axis=0, concat_axis=0, tiled=True)]
    ppermute x2 -> x0, starting transfers between devices: 8.21 us -> none  [the longest x1 6.29 us: padded(): lax.ppermute(tail, axis, [(i, (i + 1) % count) for i in range(ends)])]
    reduce_sum x30 -> x1, other arithmetic: 7.38 us -> 0.65 us  [area_weights(): return cosine / jnp.mean(cosine)]
  transfers between devices with their start and end apart: 5 -> 0, of which waited for: 4 -> 0; matrix products, arithmetic and copies ran while one was open for 3% -> 0% of each run, Pallas kernels for 0% -> 0%
where the time goes in v1:
time: 71 us; the launch traced here: 70.7 us
  Pallas kernels  61.2 us (86%)
  local copies, waits for them, and re-layouts  4.48 us (6%)
  between operations  3.05 us (4%)
  other arithmetic  1.96 us (3%)
    pallas_call x1, Pallas kernels, per_device(): pl.pallas_call(functools.partial(kernel, n_ens, n_lat), out_shape=(jax.Sh...  61.2 us
    unnamed x1, local copies, waits for them, and re-layouts  2.1 us

profile of v1, /device:TPU:1, one launch (start us, length us, event | category | flops | bytes accessed | tf_op | source)
XLA Modules:
  0.0 70.7 jit_solution(6444520215656573251)
XLA Ops:
  0.6 0.7 fusion.1
  1.9 0.6 fusion.area_ref
  2.5 0.7 reduce
  3.2 0.6 reshape.10.taps_ref
  3.8 1.1 %copy.11 = f32[1,5,5,9,5]{2,3,4,1,0:T(8,128)S(1)} copy(f32[1,5,5,9,5]{3,0,4,2,1:T(1,128)} %param.10) | data formatting | bytes 9000 | tf_op jit(solution)/shard_map/transpose | solution.py:524
  4.9 0.7 pad.4.clone
  5.6 61.2 %shard_map.77 = (f32[5,1,64,640]{3,2,1,0:T(8,128)}, f32[1]{0:T(128)}) custom-call(s32[25]{0:T(128)} %reshape.10.taps_ref, s32[5]{0:T(128)} %time_ref.1, f32[160]{0:T(256)} %fusion.area_ref, f32[5,80,5]{2,1,0:T(8,128)} %bitcast.9, f32[9,64,64]{2,1,0:T(8,128)} %bitcast.10, f32[5,1,64,640]{3,2,1,0:T(8,128)} %members_ref.1, f32[4,5,64,640]{3,2,1,0:T(8,128)} %truth_ref.1), custom_call_target="tpu_custom_call" | custom-call | flops 5000000000 | bytes 4000000 | tf_op jit(solution)/shard_map/pallas_call | solution.py:536
  66.9 2.1 %copy.14 = f32[5,1,64,640]{3,2,1,0:T(8,128)} copy(f32[5,1,64,640]{3,2,1,0:T(8,128)} %get-tuple-element.4) | data formatting | bytes 1638400

commit v2 on v1

--- a/solution.py
+++ b/solution.py
@@ -3,6 +3,7 @@
 
 import jax
 import jax.numpy as jnp
+import numpy as np
 from jax import lax
 from jax.experimental import pallas as pl
 from jax.experimental.pallas import tpu as pltpu
@@ -61,6 +62,7 @@
     own_lo,
     side_hi,
     side_lo,
+    rows_in,
     mdup,
     a_own,
     a_side,
@@ -210,23 +212,21 @@
     q_own = row_of(OWN_PAD, REACH, REACH + ROWS)
     q_sides = (row_of(SIDE, 0, REACH), row_of(SIDE, REACH + ROWS, ROWS + 2 * REACH))
 
-    def spread(r, q):
-        total = None
-        for t in range(TAPS):
-            hit = (q == taps_ref[r * TAPS + t] - first + REACH).astype(F32)
-            term = filt_ref[r, :, t : t + 1] * hit
-            total = term if total is None else total + term
-        return total
-
-    @pl.loop(0, ROWS)
-    def _(r):
-        wide = spread(r, q_own)
-        low = spread(r, q_sides[0])
-        high = spread(r, q_sides[1])
+    for i in range(ROWS * TAPS * LW):
+        rows_in[i : i + 1, :K] = filt_ref[i]
+    turned = jnp.transpose(rows_in[...])[:KP]
+
+    for r in range(ROWS):
+        hits = [
+            [(q == taps_ref[r, 0, t] - first + REACH).astype(F32) for t in range(TAPS)] for q in (q_own, *q_sides)
+        ]
         for d in range(LW):
-            a_own[r * LW + d] = wide[d * KP : (d + 1) * KP]
-            a_side[0, r * LW + d] = low[d * KP : (d + 1) * KP]
-            a_side[1, r * LW + d] = high[d * KP : (d + 1) * KP]
+            columns = [(r * TAPS + t) * LW + d for t in range(TAPS)]
+            columns = [jnp.broadcast_to(turned[:, at : at + 1], (KP, LANE)) for at in columns]
+            for ref, hit in zip((a_own, a_side.at[0], a_side.at[1]), hits):
+                for at in range(0, ref.shape[2], LANE):
+                    terms = [columns[t] * hit[t][:, at : at + LANE] for t in range(TAPS)]
+                    ref[r * LW + d, :, at : at + LANE] = functools.reduce(jnp.add, terms)
 
     def weights(rd, a_at, width):
         for at in range(0, width, LANE):
@@ -514,17 +514,16 @@
 
 
 def area_weights(total_rows):
-    latitude = (jnp.arange(total_rows, dtype=F32) + 0.5) * (math.pi / total_rows) - 0.5 * math.pi
-    cosine = jnp.cos(latitude)
-    return cosine / jnp.mean(cosine)
+    latitude = (np.arange(total_rows, dtype=np.float64) + 0.5) * (math.pi / total_rows) - 0.5 * math.pi
+    cosine = np.cos(latitude)
+    return (cosine / np.mean(cosine)).astype(np.float32)
 
 
 def per_device(n_ens, n_lat, members, truth, target_time, row_taps, filters, mixing):
-    taps = row_taps.reshape(ROWS * TAPS)
-    spread = jnp.transpose(filters[0], (0, 3, 2, 1)).reshape(1, ROWS, LW, K, TAPS)[0]
-    spread = jnp.pad(spread, ((0, 0), (0, 0), (0, KP - K), (0, 0))).reshape(ROWS, LW * KP, TAPS)
+    taps = jnp.transpose(row_taps, (1, 0, 2))
+    spread = jnp.transpose(filters, (1, 2, 4, 0, 3)).reshape(ROWS * TAPS * LW, 1, K)
     mix = jnp.transpose(mixing[0], (1, 0, 2))
-    area = area_weights(n_lat * ROWS)
+    area = jnp.asarray(area_weights(n_lat * ROWS))
     slots = BLOCKS // n_ens
     group = min(8, n_lat)
     tall = n_lat // group
@@ -533,13 +532,14 @@
     smem_spec = pl.BlockSpec(memory_space=pltpu.SMEM)
     vmem_spec = pl.BlockSpec(memory_space=pltpu.VMEM)
     any_spec = pl.BlockSpec(memory_space=pl.ANY)
+    hbm_spec = pl.BlockSpec(memory_space=pltpu.HBM)
     return pl.pallas_call(
         functools.partial(kernel, n_ens, n_lat),
         out_shape=(
             jax.ShapeDtypeStruct((ROWS, 1, C, NLON), F32),
             jax.ShapeDtypeStruct((1,), F32),
         ),
-        in_specs=[smem_spec, smem_spec, smem_spec, vmem_spec, vmem_spec, any_spec, any_spec],
+        in_specs=[smem_spec, smem_spec, smem_spec, vmem_spec, vmem_spec, hbm_spec, hbm_spec],
         out_specs=(any_spec, smem_spec),
         scratch_shapes=[
             vmem((ROWS, C, NLON), F32),
@@ -548,6 +548,7 @@
             vmem((OWN_PAD, NLON), BF16),
             vmem((SIDE, NLON), BF16),
             vmem((SIDE, NLON), BF16),
+            vmem((LANE, LANE), F32),
             vmem((K, C, LANE), F32),
             vmem((ROWS * LW, KP, OWN_PAD), F32),
             vmem((2, ROWS * LW, KP, SIDE), F32),
@@ -581,7 +582,7 @@
             dma((tall,)),
         ],
         compiler_params=pltpu.CompilerParams(
-            collective_id=0, has_side_effects=True, vmem_limit_bytes=60 * 2**20
+            collective_id=0, has_side_effects=True, vmem_limit_bytes=58 * 2**20
         ),
         cost_estimate=pl.CostEstimate(flops=5_000_000_000, bytes_accessed=4_000_000, transcendentals=400_000),
     )(taps, target_time, area, spread, mix, members, truth)

time: 71 us -> 65.7 us (0.925)
  local copies, waits for them, and re-layouts: 4.48 us -> 2.1 us
  other arithmetic: 1.96 us -> 0 us
    transpose x1 -> x0, local copies, waits for them, and re-layouts: 1.1 us -> none  [per_device(): jnp.transpose(filters[0], (0, 3, 2, 1)).reshape(1, ROWS, LW, K, TAPS)[0]]
where the time goes in v2:
time: 65.7 us; the launch traced here: 65.5 us
  Pallas kernels  61 us (93%)
  between operations  2.39 us (4%)
  local copies, waits for them, and re-layouts  2.1 us (3%)
    pallas_call x1, Pallas kernels, per_device(): pl.pallas_call(functools.partial(kernel, n_ens, n_lat), out_shape=(jax.Sh...  61 us
    unnamed x1, local copies, waits for them, and re-layouts  2.1 us

profile of v2, /device:TPU:1, one launch (start us, length us, event | category | flops | bytes accessed | tf_op | source)
XLA Modules:
  0.0 65.5 jit_solution(8886274430130227983)
XLA Ops:
  0.6 61.0 %shard_map.86 = (f32[5,1,64,640]{3,2,1,0:T(8,128)}, f32[1]{0:T(128)}) custom-call(s32[5,1,5]{2,1,0:T(1,128)} %bitcast.9, s32[5]{0:T(128)} %time_ref.1, f32[160]{0:T(256)} %constant.2.clone.area_ref, f32[125,1,9]{2,1,0:T(1,128)} %bitcast.8, f32[9,64,64]{2,1,0:T(8,128)} %bitcast.7, f32[5,1,64,640]{3,2,1,0:T(8,128)} %members_ref.1, f32[4,5,64,640]{3,2,1,0:T(8,128)} %truth_ref.1), custom_call_target="tpu_custom_call" | custom-call | flops 5000000000 | bytes 4000000 | tf_op jit(solution)/shard_map/pallas_call | solution.py:536
  61.7 2.1 %copy.11 = f32[5,1,64,640]{3,2,1,0:T(8,128)} copy(f32[5,1,64,640]{3,2,1,0:T(8,128)} %get-tuple-element.4) | data formatting | bytes 1638400

commit v3 on v2

--- a/solution.py
+++ b/solution.py
@@ -47,15 +47,20 @@
 def kernel(
     n_ens,
     n_lat,
+    taps_hbm,
+    time_hbm,
+    area_hbm,
+    filt_hbm,
+    mix_hbm,
+    members_ref,
+    truth_ref,
+    out_ref,
+    loss_ref,
     taps_ref,
     time_ref,
     area_ref,
     filt_ref,
     mix_ref,
-    members_ref,
-    truth_ref,
-    out_ref,
-    loss_ref,
     own,
     halo,
     own_hi,
@@ -76,9 +81,11 @@
     grads,
     cand,
     target,
+    pulls,
     lossbuf1,
     lossbuf2,
     lossbuf3,
+    small_sem,
     own_sem,
     cand_sem,
     halo_send,
@@ -122,23 +129,6 @@
     def outer_peer(k):
         return lax.rem(outer + k, tall) * group + inner
 
-    own_copy = pltpu.make_async_copy(members_ref.at[:, 0], own, own_sem)
-    own_copy.start()
-
-    def cand_copy(s):
-        r, lon = block_place(n_ens * s + me)
-        return pltpu.make_async_copy(
-            truth_ref.at[:, r, :, pl.ds(pl.multiple_of(lon * LANE, LANE), LANE)], cand.at[s], cand_sem.at[s]
-        )
-
-    for s in range(slots):
-        cand_copy(s).start()
-
-    @pl.when(me == extra)
-    def _():
-        r, lon = ROWS - 1, 0
-        pltpu.make_async_copy(truth_ref.at[:, r, :, pl.ds(lon, LANE)], cand.at[slots], cand_sem.at[slots]).start()
-
     barrier = pltpu.get_barrier_semaphore()
     for k in range(1, n_ens):
         pl.semaphore_signal(barrier, inc=1, device_id=place(ens_peer(k), lat), device_id_type=MESH)
@@ -156,6 +146,37 @@
     @pl.when(over_down)
     def _():
         pl.semaphore_signal(barrier, inc=1, device_id=place(me, lat - 1), device_id_type=MESH)
+
+    smalls = [
+        pltpu.make_async_copy(source, kept, small_sem.at[at])
+        for at, (source, kept) in enumerate(
+            (
+                (mix_hbm, mix_ref),
+                (filt_hbm, filt_ref),
+                (taps_hbm, taps_ref),
+                (time_hbm, time_ref),
+                (area_hbm, area_ref),
+            )
+        )
+    ]
+    for small in smalls:
+        small.start()
+    own_copy = pltpu.make_async_copy(members_ref.at[:, 0], own, own_sem)
+    own_copy.start()
+
+    def cand_copy(s):
+        r, lon = block_place(n_ens * s + me)
+        return pltpu.make_async_copy(
+            truth_ref.at[:, r, :, pl.ds(pl.multiple_of(lon * LANE, LANE), LANE)], cand.at[s], cand_sem.at[s]
+        )
+
+    for s in range(slots):
+        cand_copy(s).start()
+
+    @pl.when(me == extra)
+    def _():
+        r, lon = ROWS - 1, 0
+        pltpu.make_async_copy(truth_ref.at[:, r, :, pl.ds(lon, LANE)], cand.at[slots], cand_sem.at[slots]).start()
 
     greeted = n_ens - 1 + group - 1 + tall - 1
     pl.semaphore_wait(barrier, greeted + over_up.astype(jnp.int32) + over_down.astype(jnp.int32))
@@ -200,6 +221,9 @@
     @pl.when(jnp.logical_not(has_up))
     def _():
         halo[1] = jnp.zeros_like(halo[1])
+
+    for small in smalls:
+        small.wait()
 
     for k in range(K):
         mdup[k] = jnp.concatenate([mix_ref[k], mix_ref[k]], axis=1)
@@ -388,7 +412,7 @@
             self_sem.at[s],
         )
 
-    def score(s, b):
+    def measure(s, b):
         r, lon = block_place(b)
         for k in range(1, n_ens):
             fwd_copy(s, me, ens_peer(k)).wait_recv()
@@ -403,7 +427,6 @@
 
         zero = jnp.zeros((8, LANE), F32)
         sums = lax.fori_loop(0, C // 8, square, (zero,) * (n_ens + len(pairs)))
-        scaled = []
         skill_sum = jnp.zeros((1, LANE), F32)
         pair_sum = jnp.zeros((1, LANE), F32)
         for at, total in enumerate(sums):
@@ -411,20 +434,24 @@
             inverse = lax.rsqrt(mean)
             if at < n_ens:
                 skill_sum = skill_sum + mean * inverse
-                scaled.append(jnp.broadcast_to(inverse * area, (8, LANE)))
+                pulls[s, at] = jnp.broadcast_to(inverse * area, (8, LANE))
             else:
                 pair_sum = pair_sum + mean * inverse
-                scaled.append(jnp.broadcast_to(inverse * (area * (1.0 / n_ens)), (8, LANE)))
+                pulls[s, at] = jnp.broadcast_to(inverse * (area * (1.0 / n_ens)), (8, LANE))
         cell = skill_sum * (1.0 / n_ens) - (2.0 * pair_sum + n_ens) * (1.0 / (2 * n_ens * n_ens))
+        return jnp.broadcast_to(area * cell, (8, LANE))
+
+    def give_back(s, b):
+        r, lon = block_place(b)
 
         @pl.loop(0, C // 8)
         def _(v):
             rows = pl.ds(pl.multiple_of(v * 8, 8), 8)
             x = [recv[s, m, rows, :] for m in range(n_ens)]
             goal = target[s, rows, :]
-            g = [(x[m] - goal) * scaled[m] for m in range(n_ens)]
+            g = [(x[m] - goal) * pulls[s, m] for m in range(n_ens)]
             for at, (a, c) in enumerate(pairs):
-                pull = (x[a] - x[c]) * scaled[n_ens + at]
+                pull = (x[a] - x[c]) * pulls[s, n_ens + at]
                 g[a] = g[a] - pull
                 g[c] = g[c] + pull
             for m in range(n_ens):
@@ -433,43 +460,67 @@
         for k in range(1, n_ens):
             back_copy(s, b, r, lon, ens_peer(k)).start()
         self_copy(s, r, lon).start()
-        return jnp.broadcast_to(area * cell, (8, LANE))
-
-    part = score(0, me)
-    for s in range(1, slots):
-        part = part + score(s, n_ens * s + me)
-    lossbuf1[me] = part
-
-    @pl.when(me == extra)
-    def _():
-        recv[slots, me] = states[BLOCKS - 1]
-        lossbuf1[me] += score(slots, BLOCKS - 1)
-
-    def level(buf, send, got, count, mine, peer):
-        def copy(k, slot):
+
+    class Level:
+        def __init__(self, buf, send, got, count, mine, peer):
+            self.buf, self.send, self.got = buf, send, got
+            self.count, self.mine, self.peer = count, mine, peer
+
+        def copy(self, k, slot):
             return pltpu.make_async_remote_copy(
-                src_ref=buf.at[mine],
-                dst_ref=buf.at[slot],
-                send_sem=send.at[k],
-                recv_sem=got.at[slot],
-                device_id=peer(k),
+                src_ref=self.buf.at[self.mine],
+                dst_ref=self.buf.at[slot],
+                send_sem=self.send.at[k],
+                recv_sem=self.got.at[slot],
+                device_id=self.peer(k),
                 device_id_type=MESH,
             )
 
-        for k in range(1, count):
-            copy(k, mine).start()
-        for k in range(1, count):
-            copy(k, lax.rem(mine + k, count)).wait_recv()
-        total = buf[0]
-        for k in range(1, count):
-            total = total + buf[k]
-        return total, lambda: [copy(k, mine).wait_send() for k in range(1, count)]
-
-    total, done1 = level(lossbuf1, l1_send, l1_recv, n_ens, me, lambda k: place(ens_peer(k), lat))
-    lossbuf2[inner] = total
-    total, done2 = level(lossbuf2, l2_send, l2_recv, group, inner, lambda k: place(me, inner_peer(k)))
-    lossbuf3[outer] = total
-    total, done3 = level(lossbuf3, l3_send, l3_recv, tall, outer, lambda k: place(me, outer_peer(k)))
+        def start(self):
+            for k in range(1, self.count):
+                self.copy(k, self.mine).start()
+
+        def total(self):
+            for k in range(1, self.count):
+                self.copy(k, lax.rem(self.mine + k, self.count)).wait_recv()
+            total = self.buf[0]
+            for k in range(1, self.count):
+                total = total + self.buf[k]
+            return total
+
+        def sent(self):
+            for k in range(1, self.count):
+                self.copy(k, self.mine).wait_send()
+
+    level1 = Level(lossbuf1, l1_send, l1_recv, n_ens, me, lambda k: place(ens_peer(k), lat))
+    level2 = Level(lossbuf2, l2_send, l2_recv, group, inner, lambda k: place(me, inner_peer(k)))
+    level3 = Level(lossbuf3, l3_send, l3_recv, tall, outer, lambda k: place(me, outer_peer(k)))
+
+    part = measure(0, me)
+    give_back(0, me)
+    for s in range(1, slots):
+        part = part + measure(s, n_ens * s + me)
+    lossbuf1[me] = part
+
+    @pl.when(me == extra)
+    def _():
+        recv[slots, me] = states[BLOCKS - 1]
+        lossbuf1[me] += measure(slots, BLOCKS - 1)
+
+    level1.start()
+    give_back(1, n_ens + me)
+    lossbuf2[inner] = level1.total()
+    level2.start()
+    for s in range(2, slots):
+        give_back(s, n_ens * s + me)
+
+    @pl.when(me == extra)
+    def _():
+        give_back(slots, BLOCKS - 1)
+
+    lossbuf3[outer] = level2.total()
+    level3.start()
+    total = level3.total()
     loss_ref[0] = jnp.sum(total[0:1, :]) * (1.0 / (n_lat * ROWS * NLON))
 
     def wait_back(b, owner):
@@ -500,8 +551,8 @@
         back_copy(slots, last, *block_place(last), me).wait_recv()
         fwd_copy(slots, extra, me).wait_send()
 
-    for done in (done1, done2, done3):
-        done()
+    for level in (level1, level2, level3):
+        level.sent()
 
     def sent(side, there):
         @pl.when(there)
@@ -529,19 +580,24 @@
     tall = n_lat // group
     vmem = pltpu.VMEM
     dma = pltpu.SemaphoreType.DMA
+    smem = pltpu.SMEM
     smem_spec = pl.BlockSpec(memory_space=pltpu.SMEM)
-    vmem_spec = pl.BlockSpec(memory_space=pltpu.VMEM)
     any_spec = pl.BlockSpec(memory_space=pl.ANY)
     hbm_spec = pl.BlockSpec(memory_space=pltpu.HBM)
     return pl.pallas_call(
         functools.partial(kernel, n_ens, n_lat),
         out_shape=(
-            jax.ShapeDtypeStruct((ROWS, 1, C, NLON), F32),
+            pltpu.VMEM((ROWS, 1, C, NLON), F32),
             jax.ShapeDtypeStruct((1,), F32),
         ),
-        in_specs=[smem_spec, smem_spec, smem_spec, vmem_spec, vmem_spec, hbm_spec, hbm_spec],
+        in_specs=[hbm_spec] * 7,
         out_specs=(any_spec, smem_spec),
         scratch_shapes=[
+            smem((ROWS, 1, TAPS), jnp.int32),
+            smem((ROWS,), jnp.int32),
+            smem((n_lat * ROWS,), F32),
+            vmem((ROWS * TAPS * LW, 1, K), F32),
+            vmem((K, C, C), F32),
             vmem((ROWS, C, NLON), F32),
             vmem((2, REACH, C, NLON), F32),
             vmem((OWN_PAD, NLON), BF16),
@@ -562,9 +618,11 @@
             vmem((slots + 1, n_ens, C, LANE), F32),
             vmem((slots + 1, 4, C, LANE), F32),
             vmem((slots + 1, C, LANE), F32),
+            vmem((slots + 1, n_ens * (n_ens + 1) // 2, 8, LANE), F32),
             vmem((n_ens, 8, LANE), F32),
             vmem((group, 8, LANE), F32),
             vmem((tall, 8, LANE), F32),
+            dma((5,)),
             dma,
             dma((slots + 1,)),
             dma((2, len(CHUNKS))),
@@ -582,7 +640,7 @@
             dma((tall,)),
         ],
         compiler_params=pltpu.CompilerParams(
-            collective_id=0, has_side_effects=True, vmem_limit_bytes=58 * 2**20
+            collective_id=0, has_side_effects=True, vmem_limit_bytes=54 * 2**20
         ),
         cost_estimate=pl.CostEstimate(flops=5_000_000_000, bytes_accessed=4_000_000, transcendentals=400_000),
     )(taps, target_time, area, spread, mix, members, truth)

time: 65.7 us -> 59.7 us (0.909)
  Pallas kernels: 61 us -> 56.4 us
  local copies, waits for them, and re-layouts: 2.1 us -> 0.89 us
    pallas_call x1, Pallas kernels: 61 us -> 56.4 us  [per_device(): pl.pallas_call(functools.partial(kernel, n_ens, n_lat), out_shape=(pltpu....]
    unnamed x1, local copies, waits for them, and re-layouts: 2.1 us -> 0.89 us
where the time goes in v3:
time: 59.7 us; the launch traced here: 59.6 us
  Pallas kernels  56.4 us (94%)
  between operations  2.33 us (4%)
  local copies, waits for them, and re-layouts  0.89 us (1%)
    pallas_call x1, Pallas kernels, per_device(): pl.pallas_call(functools.partial(kernel, n_ens, n_lat), out_shape=(pltpu....  56.4 us

profile of v3, /device:TPU:1, one launch (start us, length us, event | category | flops | bytes accessed | tf_op | source)
XLA Modules:
  0.0 59.6 jit_solution(12153236263185128481)
XLA Ops:
  0.6 56.4 %shard_map.86 = (f32[5,1,64,640]{3,2,1,0:T(8,128)S(1)}, f32[1]{0:T(128)}) custom-call(s32[5,1,5]{2,1,0:T(1,128)} %bitcast.9, s32[5]{0:T(128)} %time_hbm.1, f32[160]{0:T(256)} %constant.2.clone.area_hbm, f32[125,1,9]{2,1,0:T(1,128)} %bitcast.8, f32[9,64,64]{2,1,0:T(8,128)} %bitcast.7, f32[5,1,64,640]{3,2,1,0:T(8,128)} %members_ref.1, f32[4,5,64,640]{3,2,1,0:T(8,128)} %truth_ref.1), custom_call_target="tpu_custom_call" | custom-call | flops 5000000000 | bytes 4000000 | tf_op jit(solution)/shard_map/pallas_call | solution.py:587
  57.0 0.9 %copy.11 = f32[5,1,64,640]{3,2,1,0:T(8,128)} copy(f32[5,1,64,640]{3,2,1,0:T(8,128)S(1)} %get-tuple-element.2) | data formatting | bytes 1638400

commit v4 on v3

--- a/solution.py
+++ b/solution.py
@@ -35,13 +35,13 @@
     return hi, (x - hi.astype(F32)).astype(BF16)
 
 
-def dot3(w_hi, w_lo, x_hi, x_lo):
-    dot = functools.partial(jnp.dot, preferred_element_type=F32)
-    return dot(w_hi, x_hi) + dot(w_hi, x_lo) + dot(w_lo, x_hi)
-
-
-def block_place(b):
-    return lax.rem(b, ROWS), lax.rem(b // ROWS + 1, NB)
+def dot(w, x):
+    return jnp.dot(w, x, preferred_element_type=F32)
+
+
+def place_of(core, b):
+    order = b // NB
+    return jnp.where(core == 0, ROWS - 1 - order, order), lax.rem(b, NB)
 
 
 def kernel(
@@ -63,18 +63,15 @@
     mix_ref,
     own,
     halo,
-    own_hi,
-    own_lo,
-    side_hi,
-    side_lo,
+    own_x,
+    near_x,
+    far_x,
     rows_in,
     mdup,
     a_own,
     a_side,
-    w_own_hi,
-    w_own_lo,
-    w_side_hi,
-    w_side_lo,
+    w_own,
+    w_side,
     acc,
     states,
     recv,
@@ -117,6 +114,12 @@
     has_up = lat < n_lat - 1
     has_down = lat > 0
 
+    half = n_ens // 2
+    block_place = functools.partial(place_of, core)
+
+    def block_of(s, owner):
+        return n_ens * s + lax.rem(owner, half) * 2 + owner // half
+
     def place(ens_at, lat_at):
         return {"ens": ens_at, "lat": lat_at}
 
@@ -165,38 +168,42 @@
     own_copy.start()
 
     def cand_copy(s):
-        r, lon = block_place(n_ens * s + me)
+        r, lon = block_place(block_of(s, me))
         return pltpu.make_async_copy(
             truth_ref.at[:, r, :, pl.ds(pl.multiple_of(lon * LANE, LANE), LANE)], cand.at[s], cand_sem.at[s]
         )
 
+    def extra_copy():
+        r, _ = block_place(BLOCKS - 1)
+        return pltpu.make_async_copy(
+            truth_ref.at[:, r, :, pl.ds((NB - 1) * LANE, LANE)], cand.at[slots], cand_sem.at[slots]
+        )
+
     for s in range(slots):
         cand_copy(s).start()
 
     @pl.when(me == extra)
     def _():
-        r, lon = ROWS - 1, 0
-        pltpu.make_async_copy(truth_ref.at[:, r, :, pl.ds(lon, LANE)], cand.at[slots], cand_sem.at[slots]).start()
+        extra_copy().start()
 
     greeted = n_ens - 1 + group - 1 + tall - 1
     pl.semaphore_wait(barrier, greeted + over_up.astype(jnp.int32) + over_down.astype(jnp.int32))
 
-    def halo_copy(side, chunk):
-        start, width = CHUNKS[chunk]
-        rows = pl.ds(1, REACH) if side == 0 else pl.ds(0, REACH)
+    def halo_copy(side, step):
+        row = REACH - 1 - step if side == 0 else step
         to = lat + 1 if side == 0 else lat - 1
         return pltpu.make_async_remote_copy(
-            src_ref=members_ref.at[rows, 0, :, pl.ds(start, width)],
-            dst_ref=halo.at[side, :, :, pl.ds(start, width)],
-            send_sem=halo_send.at[side, chunk],
-            recv_sem=halo_recv.at[side, chunk],
+            src_ref=members_ref.at[row + 1 - side, 0],
+            dst_ref=halo.at[side, row],
+            send_sem=halo_send.at[side, step],
+            recv_sem=halo_recv.at[side, step],
             device_id=place(me, to),
             device_id_type=MESH,
         )
 
     def send_side(side):
-        for chunk in range(len(CHUNKS)):
-            halo_copy(side, chunk).start()
+        for step in range(REACH):
+            halo_copy(side, step).start()
 
     @pl.when((core == 1) & has_up)
     def _():
@@ -213,14 +220,6 @@
     @pl.when((core == 1) & has_down)
     def _():
         send_side(1)
-
-    @pl.when(jnp.logical_not(has_down))
-    def _():
-        halo[0] = jnp.zeros_like(halo[0])
-
-    @pl.when(jnp.logical_not(has_up))
-    def _():
-        halo[1] = jnp.zeros_like(halo[1])
 
     for small in smalls:
         small.wait()
@@ -233,7 +232,7 @@
         q = low + lane // C
         return jnp.where(q < high, q, -1)
 
-    q_own = row_of(OWN_PAD, REACH, REACH + ROWS)
+    q_own = jnp.minimum(row_of(OWN_PAD, REACH, REACH + ROWS + 1), REACH + ROWS - 1)
     q_sides = (row_of(SIDE, 0, REACH), row_of(SIDE, REACH + ROWS, ROWS + 2 * REACH))
 
     for i in range(ROWS * TAPS * LW):
@@ -260,26 +259,37 @@
                 total = term if total is None else total + term
             yield at, split(total)
 
+    in_low = lax.broadcasted_iota(jnp.int32, (C, LANE), 1) < C
+
     @pl.loop(0, ROWS * LW)
     def _(rd):
         rows = pl.ds(pl.multiple_of(rd * C, C), C)
         for at, (hi, lo) in weights(rd, a_own, OWN_PAD):
-            w_own_hi[rows, at : at + LANE] = hi
-            w_own_lo[rows, at : at + LANE] = lo
+            if at < SIDE:
+                w_own[rows, at : at + LANE] = hi
+                w_own[rows, SIDE + at : SIDE + at + LANE] = hi
+                w_own[rows, 2 * SIDE + at : 2 * SIDE + at + LANE] = lo
+            else:
+                w_own[rows, 3 * SIDE : 3 * SIDE + LANE] = hi
+                w_own[rows, 3 * SIDE + LANE :] = jnp.where(in_low, lo, jnp.zeros_like(lo))
 
     own_copy.wait()
-    hi, lo = split(own[...].reshape(OWN, NLON))
-    own_hi[:OWN] = hi
-    own_lo[:OWN] = lo
-    own_hi[OWN:] = jnp.zeros((OWN_PAD - OWN, NLON), BF16)
-    own_lo[OWN:] = jnp.zeros((OWN_PAD - OWN, NLON), BF16)
+    hi, lo = split(own[:REACH].reshape(SIDE, NLON))
+    own_x[:SIDE] = hi
+    own_x[SIDE : 2 * SIDE] = lo
+    own_x[2 * SIDE : 3 * SIDE] = hi
+    hi, lo = split(own[REACH])
+    own_x[3 * SIDE : 3 * SIDE + C] = hi
+    own_x[3 * SIDE + C : 3 * SIDE + 2 * C] = lo
+    own_x[3 * SIDE + 2 * C : 3 * SIDE + 3 * C] = hi
+    own_x[3 * SIDE + 3 * C :] = jnp.zeros((C, NLON), BF16)
 
     @pl.loop(0, ROWS)
     def _(r):
         rows = pl.ds(pl.multiple_of(r * BAND, BAND), BAND)
         for start, width in CHUNKS:
             lons = pl.ds(start, width)
-            acc[rows, lons] = dot3(w_own_hi[rows, :], w_own_lo[rows, :], own_hi[:, lons], own_lo[:, lons])
+            acc[rows, lons] = dot(w_own[rows, :], own_x[:, lons])
 
     def side_weights(side):
         a_at = a_side.at[side]
@@ -288,35 +298,35 @@
         def _(i):
             rows = pl.ds(pl.multiple_of(i * C, C), C)
             for at, (hi, lo) in weights(i + side * LW, a_at, SIDE):
-                w_side_hi[rows, at : at + LANE] = hi
-                w_side_lo[rows, at : at + LANE] = lo
-
-    def wait_halo(side, chunk):
-        @pl.when((side == 0) & has_down)
+                w_side[rows, at : at + LANE] = hi
+                w_side[rows, SIDE + at : SIDE + at + LANE] = hi
+                w_side[rows, 2 * SIDE + at : 2 * SIDE + at + LANE] = lo
+
+    def add_row(side, i, x_ref):
+        rows = pl.ds(pl.multiple_of(i * BAND, BAND), BAND)
+        acc_rows = pl.ds(pl.multiple_of((i + side) * BAND, BAND), BAND)
+        for start, width in CHUNKS:
+            lons = pl.ds(start, width)
+            acc[acc_rows, lons] += dot(w_side[rows, :], x_ref[:, lons])
+
+    side_weights(near)
+    far_x[...] = jnp.zeros_like(far_x)
+    for side in range(2):
+
+        @pl.when(near == side)
         def _():
-            halo_copy(0, chunk).wait_recv()
-
-        @pl.when((side == 1) & has_up)
-        def _():
-            halo_copy(1, chunk).wait_recv()
-
-    def add_side(side, chunk):
-        start, width = CHUNKS[chunk]
-        lons = pl.ds(start, width)
-        hi, lo = split(halo[side, :, :, lons].reshape(SIDE, width))
-        side_hi[:, lons] = hi
-        side_lo[:, lons] = lo
-
-        @pl.loop(0, REACH)
-        def _(i):
-            rows = pl.ds(pl.multiple_of(i * BAND, BAND), BAND)
-            acc_rows = pl.ds(pl.multiple_of((i + side) * BAND, BAND), BAND)
-            acc[acc_rows, lons] += dot3(w_side_hi[rows, :], w_side_lo[rows, :], side_hi[:, lons], side_lo[:, lons])
-
-    side_weights(near)
-    for chunk in range(len(CHUNKS)):
-        wait_halo(near, chunk)
-        add_side(near, chunk)
+            for step in range(REACH):
+                halo_copy(side, step).wait_recv()
+
+    hi, lo = split(halo[near].reshape(SIDE, NLON))
+    near_x[:SIDE] = hi
+    near_x[SIDE : 2 * SIDE] = lo
+    near_x[2 * SIDE :] = hi
+
+    @pl.loop(0, REACH)
+    def _(i):
+        add_row(near, i, near_x)
+
     side_weights(far)
 
     def pick_target(s, r):
@@ -328,37 +338,39 @@
 
     for s in range(slots):
         cand_copy(s).wait()
-        pick_target(s, lax.rem(n_ens * s + me, ROWS))
+        pick_target(s, block_place(block_of(s, me))[0])
 
     @pl.when(me == extra)
     def _():
-        pltpu.make_async_copy(truth_ref.at[:, ROWS - 1, :, pl.ds(0, LANE)], cand.at[slots], cand_sem.at[slots]).wait()
-        pick_target(slots, ROWS - 1)
+        extra_copy().wait()
+        pick_target(slots, block_place(BLOCKS - 1)[0])
 
     lane = lax.broadcasted_iota(jnp.int32, (C, LANE), 1)
 
-    def finish(lon, first_block):
-        @pl.loop(0, ROWS)
-        def _(r):
-            def part(d, at):
-                rows = pl.ds(pl.multiple_of(r * BAND + d * C, C), C)
-                return acc[rows, at * LANE : (at + 1) * LANE]
-
+    def finish(order):
+        r, _ = block_place(order * NB)
+
+        def part(d, at):
+            rows = pl.ds(pl.multiple_of(r * BAND + d * C, C), C)
+            at = at % NB
+            return acc[rows, at * LANE : (at + 1) * LANE]
+
+        for lon in range(NB):
             total = part(2, lon)
             for d in (0, 1, 3, 4):
                 shift = d - LW // 2
                 if shift > 0:
-                    mine = jnp.where(lane < shift, part(d, (lon + 1) % NB), part(d, lon))
+                    mine = jnp.where(lane < shift, part(d, lon + 1), part(d, lon))
                 else:
-                    mine = jnp.where(lane >= LANE + shift, part(d, (lon - 1) % NB), part(d, lon))
+                    mine = jnp.where(lane >= LANE + shift, part(d, lon - 1), part(d, lon))
                 total = total + pltpu.roll(mine, (-shift) % LANE, 1)
             cube = total + 0.044715 * total * total * total
             gelu = 0.5 * total * (1.0 + jnp.tanh(math.sqrt(2.0 / math.pi) * cube))
-            states[first_block + r] = own[r, :, lon * LANE : (lon + 1) * LANE] + gelu
+            states[order * NB + lon] = own[r, :, lon * LANE : (lon + 1) * LANE] + gelu
 
     def fwd_copy(s, to, source):
         return pltpu.make_async_remote_copy(
-            src_ref=states.at[n_ens * s + to] if s < slots else states.at[BLOCKS - 1],
+            src_ref=states.at[block_of(s, to)] if s < slots else states.at[BLOCKS - 1],
             dst_ref=recv.at[s, source],
             send_sem=fwd_send.at[s, to],
             recv_sem=fwd_recv.at[s, source],
@@ -366,32 +378,36 @@
             device_id_type=MESH,
         )
 
-    def send_slot(s):
-        for k in range(1, n_ens):
-            fwd_copy(s, ens_peer(k), me).start()
-        recv[s, me] = states[n_ens * s + me]
-
-    for chunk in (0, 1):
-        wait_halo(far, chunk)
-        add_side(far, chunk)
-    finish(1, 0)
-    finish(2, 5)
-    send_slot(0)
-    wait_halo(far, 2)
-    add_side(far, 2)
-    finish(3, 10)
-    for s in range(1, slots):
-        if n_ens * (s + 1) <= 15:
-            send_slot(s)
-    finish(4, 15)
-    finish(0, 20)
-    for s in range(1, slots):
-        if n_ens * (s + 1) > 15:
-            send_slot(s)
-
-    @pl.when(me != extra)
-    def _():
-        fwd_copy(slots, extra, me).start()
+    def send_row(order):
+        for b in range(order * NB, (order + 1) * NB):
+            s, j = divmod(b, n_ens)
+            to = j % 2 * half + j // 2 if s < slots else extra
+
+            @pl.when(me != to)
+            def _():
+                fwd_copy(s, to, me).start()
+
+            @pl.when(me == to)
+            def _():
+                recv[s, me] = states[b]
+
+    finish(0)
+    send_row(0)
+    for step in range(REACH):
+        for side, there in ((0, has_down), (1, has_up)):
+
+            @pl.when((far == side) & there)
+            def _():
+                halo_copy(side, step).wait_recv()
+                row = REACH - 1 - step if side == 0 else step
+                hi, lo = split(halo[side, row])
+                far_x[row * C : (row + 1) * C] = hi
+                far_x[SIDE + row * C : SIDE + (row + 1) * C] = lo
+                far_x[2 * SIDE + row * C : 2 * SIDE + (row + 1) * C] = hi
+
+        add_row(far, jnp.where(far == 0, REACH - 1 - step, step), far_x)
+        finish(step + 1)
+        send_row(step + 1)
 
     pairs = [(a, b) for a in range(n_ens) for b in range(a + 1, n_ens)]
 
@@ -496,45 +512,37 @@
     level2 = Level(lossbuf2, l2_send, l2_recv, group, inner, lambda k: place(me, inner_peer(k)))
     level3 = Level(lossbuf3, l3_send, l3_recv, tall, outer, lambda k: place(me, outer_peer(k)))
 
-    part = measure(0, me)
-    give_back(0, me)
-    for s in range(1, slots):
-        part = part + measure(s, n_ens * s + me)
-    lossbuf1[me] = part
+    part = measure(0, block_of(0, me))
+    give_back(0, block_of(0, me))
+    part = part + measure(1, block_of(1, me))
+    part = part + measure(2, block_of(2, me))
+    lossbuf2[inner] = part
 
     @pl.when(me == extra)
     def _():
-        recv[slots, me] = states[BLOCKS - 1]
-        lossbuf1[me] += measure(slots, BLOCKS - 1)
-
-    level1.start()
-    give_back(1, n_ens + me)
-    lossbuf2[inner] = level1.total()
+        lossbuf2[inner] += measure(slots, BLOCKS - 1)
+
     level2.start()
-    for s in range(2, slots):
-        give_back(s, n_ens * s + me)
-
-    @pl.when(me == extra)
-    def _():
-        give_back(slots, BLOCKS - 1)
-
+    give_back(1, block_of(1, me))
     lossbuf3[outer] = level2.total()
     level3.start()
-    total = level3.total()
+    give_back(2, block_of(2, me))
+
+    @pl.when(me == extra)
+    def _():
+        give_back(slots, BLOCKS - 1)
+
+    lossbuf1[me] = level3.total()
+    level1.start()
+    total = level1.total()
     loss_ref[0] = jnp.sum(total[0:1, :]) * (1.0 / (n_lat * ROWS * NLON))
 
-    def wait_back(b, owner):
-        @pl.when(me != owner)
-        def _():
-            r, lon = block_place(b)
-            back_copy(0, b, r, lon, me).wait_recv()
-
     for s in range(slots):
-        b = n_ens * s + me
+        b = block_of(s, me)
         self_copy(s, *block_place(b)).wait()
         for k in range(1, n_ens):
             to = ens_peer(k)
-            c = n_ens * s + to
+            c = block_of(s, to)
             back_copy(s, c, *block_place(c), me).wait_recv()
             back_copy(s, b, *block_place(b), to).wait_send()
             fwd_copy(s, to, me).wait_send()
@@ -557,8 +565,8 @@
     def sent(side, there):
         @pl.when(there)
         def _():
-            for chunk in range(len(CHUNKS)):
-                halo_copy(side, chunk).wait_send()
+            for step in range(REACH):
+                halo_copy(side, step).wait_send()
 
     sent(0, has_up)
     sent(1, has_down)
@@ -600,18 +608,15 @@
             vmem((K, C, C), F32),
             vmem((ROWS, C, NLON), F32),
             vmem((2, REACH, C, NLON), F32),
-            vmem((OWN_PAD, NLON), BF16),
-            vmem((OWN_PAD, NLON), BF16),
-            vmem((SIDE, NLON), BF16),
-            vmem((SIDE, NLON), BF16),
+            vmem((4 * SIDE, NLON), BF16),
+            vmem((3 * SIDE, NLON), BF16),
+            vmem((3 * SIDE, NLON), BF16),
             vmem((LANE, LANE), F32),
             vmem((K, C, LANE), F32),
             vmem((ROWS * LW, KP, OWN_PAD), F32),
             vmem((2, ROWS * LW, KP, SIDE), F32),
-            vmem((ROWS * BAND, OWN_PAD), BF16),
-            vmem((ROWS * BAND, OWN_PAD), BF16),
-            vmem((REACH * BAND, SIDE), BF16),
-            vmem((REACH * BAND, SIDE), BF16),
+            vmem((ROWS * BAND, 4 * SIDE), BF16),
+            vmem((REACH * BAND, 3 * SIDE), BF16),
             vmem((ROWS * BAND, NLON), F32),
             vmem((BLOCKS, C, LANE), F32),
             vmem((slots + 1, n_ens, C, LANE), F32),
@@ -625,8 +630,8 @@
             dma((5,)),
             dma,
             dma((slots + 1,)),
-            dma((2, len(CHUNKS))),
-            dma((2, len(CHUNKS))),
+            dma((2, REACH)),
+            dma((2, REACH)),
             dma((slots + 1, n_ens)),
             dma((slots + 1, n_ens)),
             dma((slots + 1, n_ens)),

time: 59.7 us -> 54.9 us (0.920)
  Pallas kernels: 56.4 us -> 51.6 us
    pallas_call x1, Pallas kernels: 56.4 us -> 51.6 us  [per_device(): pl.pallas_call(functools.partial(kernel, n_ens, n_lat), out_shape=(pltpu....]
where the time goes in v4:
time: 54.9 us; the launch traced here: 54.8 us
  Pallas kernels  51.6 us (94%)
  between operations  2.33 us (4%)
  local copies, waits for them, and re-layouts  0.89 us (2%)
    pallas_call x1, Pallas kernels, per_device(): pl.pallas_call(functools.partial(kernel, n_ens, n_lat), out_shape=(pltpu....  51.6 us

profile of v4, /device:TPU:1, one launch (start us, length us, event | category | flops | bytes accessed | tf_op | source)
XLA Modules:
  0.0 54.8 jit_solution(3574452432406459484)
XLA Ops:
  0.6 51.6 %shard_map.86 = (f32[5,1,64,640]{3,2,1,0:T(8,128)S(1)}, f32[1]{0:T(128)}) custom-call(s32[5,1,5]{2,1,0:T(1,128)} %bitcast.9, s32[5]{0:T(128)} %time_hbm.1, f32[160]{0:T(256)} %constant.2.clone.area_hbm, f32[125,1,9]{2,1,0:T(1,128)} %bitcast.8, f32[9,64,64]{2,1,0:T(8,128)} %bitcast.7, f32[5,1,64,640]{3,2,1,0:T(8,128)} %members_ref.1, f32[4,5,64,640]{3,2,1,0:T(8,128)} %truth_ref.1), custom_call_target="tpu_custom_call" | custom-call | flops 5000000000 | bytes 4000000 | tf_op jit(solution)/shard_map/pallas_call | solution.py:595
  52.2 0.9 %copy.11 = f32[5,1,64,640]{3,2,1,0:T(8,128)} copy(f32[5,1,64,640]{3,2,1,0:T(8,128)S(1)} %get-tuple-element.2) | data formatting | bytes 1638400

commit v5 on v4

--- a/solution.py
+++ b/solution.py
@@ -37,6 +37,10 @@
 
 def dot(w, x):
     return jnp.dot(w, x, preferred_element_type=F32)
+
+
+def far_first(count):
+    return sorted(range(1, count), key=lambda k: -min(k, count - k))
 
 
 def place_of(core, b):
@@ -133,10 +137,10 @@
         return lax.rem(outer + k, tall) * group + inner
 
     barrier = pltpu.get_barrier_semaphore()
-    for k in range(1, n_ens):
+    for k in far_first(group):
+        pl.semaphore_signal(barrier, inc=1, device_id=place(me, inner_peer(k)), device_id_type=MESH)
+    for k in far_first(n_ens):
         pl.semaphore_signal(barrier, inc=1, device_id=place(ens_peer(k), lat), device_id_type=MESH)
-    for k in range(1, group):
-        pl.semaphore_signal(barrier, inc=1, device_id=place(me, inner_peer(k)), device_id_type=MESH)
     for k in range(1, tall):
         pl.semaphore_signal(barrier, inc=1, device_id=place(me, outer_peer(k)), device_id_type=MESH)
     over_up = has_up & (inner == group - 1)
@@ -347,6 +351,28 @@
 
     lane = lax.broadcasted_iota(jnp.int32, (C, LANE), 1)
 
+    def fwd_copy(s, to, source):
+        return pltpu.make_async_remote_copy(
+            src_ref=states.at[block_of(s, to)] if s < slots else states.at[BLOCKS - 1],
+            dst_ref=recv.at[s, source],
+            send_sem=fwd_send.at[s, to],
+            recv_sem=fwd_recv.at[s, source],
+            device_id=place(to, lat),
+            device_id_type=MESH,
+        )
+
+    def send_block(b):
+        s, j = divmod(b, n_ens)
+        to = j % 2 * half + j // 2 if s < slots else extra
+
+        @pl.when(me != to)
+        def _():
+            fwd_copy(s, to, me).start()
+
+        @pl.when(me == to)
+        def _():
+            recv[s, me] = states[b]
+
     def finish(order):
         r, _ = block_place(order * NB)
 
@@ -367,32 +393,9 @@
             cube = total + 0.044715 * total * total * total
             gelu = 0.5 * total * (1.0 + jnp.tanh(math.sqrt(2.0 / math.pi) * cube))
             states[order * NB + lon] = own[r, :, lon * LANE : (lon + 1) * LANE] + gelu
-
-    def fwd_copy(s, to, source):
-        return pltpu.make_async_remote_copy(
-            src_ref=states.at[block_of(s, to)] if s < slots else states.at[BLOCKS - 1],
-            dst_ref=recv.at[s, source],
-            send_sem=fwd_send.at[s, to],
-            recv_sem=fwd_recv.at[s, source],
-            device_id=place(to, lat),
-            device_id_type=MESH,
-        )
-
-    def send_row(order):
-        for b in range(order * NB, (order + 1) * NB):
-            s, j = divmod(b, n_ens)
-            to = j % 2 * half + j // 2 if s < slots else extra
-
-            @pl.when(me != to)
-            def _():
-                fwd_copy(s, to, me).start()
-
-            @pl.when(me == to)
-            def _():
-                recv[s, me] = states[b]
+            send_block(order * NB + lon)
 
     finish(0)
-    send_row(0)
     for step in range(REACH):
         for side, there in ((0, has_down), (1, has_up)):
 
@@ -407,7 +410,6 @@
 
         add_row(far, jnp.where(far == 0, REACH - 1 - step, step), far_x)
         finish(step + 1)
-        send_row(step + 1)
 
     pairs = [(a, b) for a in range(n_ens) for b in range(a + 1, n_ens)]
 
@@ -473,7 +475,7 @@
             for m in range(n_ens):
                 grads[s, m, rows, :] = g[m]
 
-        for k in range(1, n_ens):
+        for k in far_first(n_ens):
             back_copy(s, b, r, lon, ens_peer(k)).start()
         self_copy(s, r, lon).start()
 
@@ -493,7 +495,7 @@
             )
 
         def start(self):
-            for k in range(1, self.count):
+            for k in far_first(self.count):
                 self.copy(k, self.mine).start()
 
         def total(self):

time: 54.9 us -> 55 us (level)
  no operation moved by 1% of the time
where the time goes in v5:
time: 55 us; the launch traced here: 54.9 us
  Pallas kernels  51.6 us (94%)
  between operations  2.33 us (4%)
  local copies, waits for them, and re-layouts  0.89 us (2%)
    pallas_call x1, Pallas kernels, per_device(): pl.pallas_call(functools.partial(kernel, n_ens, n_lat), out_shape=(pltpu....  51.6 us

profile of v5, /device:TPU:1, one launch (start us, length us, event | category | flops | bytes accessed | tf_op | source)
XLA Modules:
  0.0 54.9 jit_solution(8587405671354303944)
XLA Ops:
  0.6 51.6 %shard_map.86 = (f32[5,1,64,640]{3,2,1,0:T(8,128)S(1)}, f32[1]{0:T(128)}) custom-call(s32[5,1,5]{2,1,0:T(1,128)} %bitcast.9, s32[5]{0:T(128)} %time_hbm.1, f32[160]{0:T(256)} %constant.2.clone.area_hbm, f32[125,1,9]{2,1,0:T(1,128)} %bitcast.8, f32[9,64,64]{2,1,0:T(8,128)} %bitcast.7, f32[5,1,64,640]{3,2,1,0:T(8,128)} %members_ref.1, f32[4,5,64,640]{3,2,1,0:T(8,128)} %truth_ref.1), custom_call_target="tpu_custom_call" | custom-call | flops 5000000000 | bytes 4000000 | tf_op jit(solution)/shard_map/pallas_call | solution.py:597
  52.3 0.9 %copy.11 = f32[5,1,64,640]{3,2,1,0:T(8,128)} copy(f32[5,1,64,640]{3,2,1,0:T(8,128)S(1)} %get-tuple-element.2) | data formatting | bytes 1638400

commit v6 on v5

--- a/solution.py
+++ b/solution.py
@@ -381,7 +381,7 @@
             at = at % NB
             return acc[rows, at * LANE : (at + 1) * LANE]
 
-        for lon in range(NB):
+        for lon in ((4, 0, 1, 2, 3) if order == ROWS - 1 else range(NB)):
             total = part(2, lon)
             for d in (0, 1, 3, 4):
                 shift = d - LW // 2

time: 55 us -> 54.7 us (level)
  no operation moved by 1% of the time
where the time goes in v6:
time: 54.7 us; the launch traced here: 54.6 us
  Pallas kernels  51.4 us (94%)
  between operations  2.33 us (4%)
  local copies, waits for them, and re-layouts  0.89 us (2%)
    pallas_call x1, Pallas kernels, per_device(): pl.pallas_call(functools.partial(kernel, n_ens, n_lat), out_shape=(pltpu....  51.4 us

profile of v6, /device:TPU:1, one launch (start us, length us, event | category | flops | bytes accessed | tf_op | source)
XLA Modules:
  0.0 54.6 jit_solution(17349022160750967572)
XLA Ops:
  0.6 51.4 %shard_map.86 = (f32[5,1,64,640]{3,2,1,0:T(8,128)S(1)}, f32[1]{0:T(128)}) custom-call(s32[5,1,5]{2,1,0:T(1,128)} %bitcast.9, s32[5]{0:T(128)} %time_hbm.1, f32[160]{0:T(256)} %constant.2.clone.area_hbm, f32[125,1,9]{2,1,0:T(1,128)} %bitcast.8, f32[9,64,64]{2,1,0:T(8,128)} %bitcast.7, f32[5,1,64,640]{3,2,1,0:T(8,128)} %members_ref.1, f32[4,5,64,640]{3,2,1,0:T(8,128)} %truth_ref.1), custom_call_target="tpu_custom_call" | custom-call | flops 5000000000 | bytes 4000000 | tf_op jit(solution)/shard_map/pallas_call | solution.py:597
  52.0 0.9 %copy.11 = f32[5,1,64,640]{3,2,1,0:T(8,128)} copy(f32[5,1,64,640]{3,2,1,0:T(8,128)S(1)} %get-tuple-element.2) | data formatting | bytes 1638400
